TPU v7x, 256 devices: a whole 4x4x8 slice. The times are simulated.
256 devices in a mesh: gz: 4 (over z_hi), gy: 8 (over x, core), gx: 8 (over z_lo, y).
Axes of the slice: x: 4, y: 4, z: 8 (z_hi: 4, z_lo: 2; z = z_hi * 2 + z_lo), core: 2. Of those that a mesh axis runs over, the one named last changes fastest.
Arguments:
- cotangent: bfloat16 [4, 128, 128, 384], P('gz', 'gy', 'gx'), may hold values from -6 to 6
- saved_codes: bfloat16 [3, 4, 128, 128, 384], P(None, 'gz', 'gy', 'gx'), may hold values from -448 to 448
- saved_scales: bfloat16 [3, 4, 128, 128, 3], P(None, 'gz', 'gy', 'gx'), may hold values from 0.0039978027 to 0.049804688
- gains: float32 [3, 384], replicated, may hold values from 0.1 to 1.9
- w_qkv: bfloat16 [3, 384, 1152], replicated, may hold values from -1 to 1
- w_out: bfloat16 [3, 384, 384], replicated, may hold values from -0.3125 to 0.3125
Outputs:
- grad_input: bfloat16 [4, 128, 128, 384], P('gz', 'gy', 'gx')
- weight_grads: float32 [1536, 1152], P(('gz', 'gy', 'gx'))
All inputs are finite; a program needn't handle non-finite values.
Results may differ from a plain program's by a relative error of at most 0.015.
Values may be sent and summed in bfloat16 or wider, within the bound.
No kernel may reach another device: no remote copies, remote signals or barrier semaphores. Data moves between devices by JAX's collectives and lax.ppermute only.
A program may use at most 128 MiB of HBM per device.

v0:
```python
import functools
import math

import jax
import jax.numpy as jnp
import numpy as np
from jax import lax
from jax.experimental import pallas as pl
from jax.experimental.pallas import tpu as pltpu
from jax.sharding import PartitionSpec as P

C = 384
T = 256
BF = jnp.bfloat16
F32 = jnp.float32
VMEM = 60 * 1024 * 1024


def one_hot_rows(source):
    m = np.zeros((len(source), len(source)), np.float32)
    m[np.arange(len(source)), source] = 1.0
    return m


def token_orders():
    n = np.arange(T)
    to_rows = ((n % 32) // 2) * 16 + 2 * (n // 32) + n % 2
    j, i, r, c = n // 32, (n // 4) % 8, (n // 2) % 2, n % 2
    cols = i * 32 + r * 16 + 2 * j + c
    to_cols = np.zeros((2 * T, T), np.float32)
    to_cols[8 * (n // 4) + n % 4, cols] = 1.0
    from_cols = np.zeros((T, 2 * T), np.float32)
    from_cols[n, 8 * (n // 4) + n % 4] = 1.0
    z, j, r, c = n // 64, (n // 8) % 8, (n // 2) % 4, n % 2
    to_depth = j * 32 + z * 8 + r * 2 + c
    z, r, j, c = n // 64, (n // 16) % 4, (n // 2) % 8, n % 2
    to_home = z * 64 + j * 8 + r * 2 + c
    return [one_hot_rows(to_rows), to_cols, from_cols, one_hot_rows(to_depth), one_hot_rows(to_home)]


def mm(a, b):
    return jnp.dot(a, b, preferred_element_type=F32)


def mm_nt(a, b):
    return lax.dot_general(a, b, (((1,), (1,)), ((), ())), preferred_element_type=F32)


def mm_tn(a, b):
    return lax.dot_general(a, b, (((0,), (0,)), ((), ())), preferred_element_type=F32)


def line_bias(layer):
    q = lax.broadcasted_iota(jnp.int32, (T, T), 0)
    k = lax.broadcasted_iota(jnp.int32, (T, T), 1)
    bits = {2: 16, 1: 1, 0: 63}[layer]
    return jnp.where((q & bits) == (k & bits), 0.0, -1e30).astype(F32)


def head_masks():
    lane = lax.broadcasted_iota(jnp.int32, (1, 128), 1)
    low = jnp.where(lane < 64, 1.0, 0.0).astype(F32)
    return low.astype(BF), (1.0 - low).astype(BF)


def normalise(y):
    y = y.astype(F32)
    rstd = lax.rsqrt(jnp.mean(y * y, axis=-1, keepdims=True) + 1e-05)
    return y * rstd, rstd


def forward(layer, y, gain, w_qkv, probs_ref):
    x_hat, _ = normalise(y)
    normed = (x_hat * gain).astype(BF)
    qkv = mm(normed, w_qkv).astype(BF)
    queries = qkv[:, :C] * jnp.asarray(0.125, BF)
    bias = line_bias(layer)
    masks = head_masks()
    attended = []
    for p in range(3):
        at = slice(128 * p, 128 * p + 128)
        q2, k2, v2 = queries[:, at], qkv[:, C:2 * C][:, at], qkv[:, 2 * C:][:, at]
        out = None
        for side in range(2):
            scores = mm_nt(q2 * masks[side], k2) + bias
            top = jnp.max(scores, axis=-1, keepdims=True)
            e = jnp.exp(scores - top)
            probs = e * (1.0 / jnp.sum(e, axis=-1, keepdims=True))
            low = probs.astype(BF)
            probs_ref[2 * p + side] = low
            part = mm(low, v2 * masks[side])
            out = part if out is None else out + part
        attended.append(out.astype(BF))
    return normed, queries, qkv[:, C:2 * C], qkv[:, 2 * C:], jnp.concatenate(attended, axis=1)


def backward_attention(stream, w_out, queries, keys, values, probs_ref):
    grad_attended = mm_nt(stream, w_out).astype(BF)
    masks = head_masks()
    dq, dk, dv = [], [], []
    for p in range(3):
        at = slice(128 * p, 128 * p + 128)
        q2, k2, v2, g2 = queries[:, at], keys[:, at], values[:, at], grad_attended[:, at]
        sums = None
        for side in range(2):
            low = probs_ref[2 * p + side]
            g = g2 * masks[side]
            probs = low.astype(F32)
            dprobs = mm_nt(g, v2)
            weighted = probs * dprobs
            total = jnp.sum(weighted, axis=-1, keepdims=True)
            dscore = (weighted - probs * total).astype(BF)
            new = (
                mm(dscore, k2 * masks[side]),
                mm_tn(dscore, q2 * masks[side]),
                mm_tn(low, g),
            )
            sums = new if sums is None else tuple(a + b for a, b in zip(sums, new))
        dq.append((sums[0] * 0.125).astype(BF))
        dk.append(sums[1].astype(BF))
        dv.append(sums[2].astype(BF))
    return [jnp.concatenate(d, axis=1) for d in (dq, dk, dv)]


def backward_input(y, stream, gain, w_qkv, parts):
    grad_normed = mm_nt(parts[0], w_qkv[:, :C])
    grad_normed += mm_nt(parts[1], w_qkv[:, C:2 * C])
    grad_normed += mm_nt(parts[2], w_qkv[:, 2 * C:])
    x_hat, rstd = normalise(y)
    d = grad_normed * gain
    branch = rstd * (
        d
        - jnp.mean(d, axis=-1, keepdims=True)
        - x_hat * jnp.mean(d * x_hat, axis=-1, keepdims=True)
    )
    return (stream.astype(F32) + branch).astype(BF)


def weight_terms(parts, normed, stream, attended, keep_ref, send_ref):
    me = lax.axis_index("gy")
    core, x = me % 2, me // 2
    for n, (rows, cols) in enumerate(
        [(parts[0], normed), (parts[1], normed), (parts[2], normed), (stream, attended)]
    ):
        term = mm_tn(rows, cols).astype(BF)
        for j in range(8):
            block = term[48 * j:48 * j + 48]
            slot = (j // 2 + 4 - x) % 4
            at = (slot, slice(48 * n, 48 * n + 48))

            @pl.when((j % 2) == core)
            def _():
                keep_ref[at] = block

            @pl.when((j % 2) != core)
            def _():
                send_ref[at] = block


def place(index, count):
    return pl.ds(pl.multiple_of(count * index, count), count)


def centre_kernel(codes, scales, cot, order, first_ref, *refs):
    token = lax.broadcasted_iota(jnp.int32, (T, 16), 0)
    lane = lax.broadcasted_iota(jnp.int32, (T, 16), 1)
    row_of = jnp.where(token // 16 == lane, 1.0, 0.0).astype(BF)
    col_of = jnp.where(token % 16 == lane, 1.0, 0.0).astype(F32)
    ones = jnp.ones((16, 128), BF)

    def centred(layer):
        blocks = []
        for b in range(3):
            own = (mm(row_of, scales[3 * layer + b]) * col_of).astype(BF)
            blocks.append(codes[layer, :, 128 * b:128 * b + 128].astype(F32) * mm(own, ones))
        h = jnp.concatenate(blocks, axis=1)
        return (h - jnp.mean(h, axis=-1, keepdims=True)).astype(BF)

    first_ref[:, :C] = centred(2)
    first_ref[:, C:] = cot[...]
    both = jnp.concatenate([centred(1), centred(0)], axis=1)
    refs[-1][...] = mm(order[...], both).astype(BF)
    me = lax.axis_index("gy")
    for step in range(8):
        refs[step][...] = refs[-1][place(me ^ step, 32), :]


def column_kernel(x, gains, w_qkv, w_out, order, *refs):
    stream_ref, saved_ref, probs_ref = refs[-3:]
    gain, wq, wo = gains[2:3, :], w_qkv[0], w_out[0]
    y, stream = x[:, :C], x[:, C:]
    normed, queries, keys, values, attended = forward(2, y, gain, wq, probs_ref)
    parts = backward_attention(stream, wo, queries, keys, values, probs_ref)
    new = backward_input(y, stream, gain, wq, parts)
    stream_ref[...] = mm(order[...], new).astype(BF)
    saved_ref[:, :C] = normed
    saved_ref[:, C:2 * C] = attended
    for n in range(3):
        saved_ref[:, (2 + n) * C:(3 + n) * C] = parts[n]


def row_forward_kernel(*refs):
    gains, w_qkv, saved_ref, probs_ref, x_ref = refs[8:]
    me = lax.axis_index("gy")
    for step in range(8):
        x_ref[place(me ^ step, 32), :] = refs[step][...]
    normed, queries, keys, values, attended = forward(1, x_ref[:, :C], gains[1:2, :], w_qkv[0], probs_ref)
    for n, v in enumerate((normed, attended, queries, keys, values)):
        saved_ref[:, n * C:(n + 1) * C] = v


def row_backward_kernel(x, got, saved, probs, gains, w_qkv, w_out, from_cols, order, both_ref, parts_ref, stream_ref):
    stream = mm(from_cols[...], got[...]).astype(BF)
    stream_ref[...] = stream
    parts = backward_attention(
        stream, w_out[0], saved[:, 2 * C:3 * C], saved[:, 3 * C:4 * C], saved[:, 4 * C:], probs
    )
    new = backward_input(x[:, :C], stream, gains[1:2, :], w_qkv[0], parts)
    both_ref[...] = mm(order[...], jnp.concatenate([x[:, C:], new], axis=1)).astype(BF)
    for n in range(3):
        parts_ref[:, n * C:(n + 1) * C] = parts[n]


def column_weight_kernel(saved, stream, keep_ref, send_ref):
    pieces = [saved[:, (2 + n) * C:(3 + n) * C] for n in range(3)]
    weight_terms(pieces, saved[:, :C], stream[...], saved[:, C:2 * C], keep_ref, send_ref)


def row_weight_kernel(saved, parts, stream, keep_ref, send_ref):
    pieces = [parts[:, n * C:(n + 1) * C] for n in range(3)]
    weight_terms(pieces, saved[:, :C], stream[...], saved[:, C:2 * C], keep_ref, send_ref)


def depth_kernel(x, gains, w_qkv, w_out, *refs):
    grad_ref, keep_ref, send_ref, probs_ref = refs[-4:]
    gain, wq, wo = gains[0:1, :], w_qkv[0], w_out[0]
    y, stream = x[:, :C], x[:, C:]
    normed, queries, keys, values, attended = forward(0, y, gain, wq, probs_ref)
    parts = backward_attention(stream, wo, queries, keys, values, probs_ref)
    weight_terms(parts, normed, stream, attended, keep_ref, send_ref)
    grad_ref[...] = backward_input(y, stream, gain, wq, parts)


def home_kernel(x, order, out_ref):
    out_ref[...] = mm(order[...], x[...]).astype(BF)


MAIN = 7 * 128


def sum_kernel(*refs):
    terms, out_ref = refs[:15], refs[15]
    sums = []
    for layer in range(3):
        total = terms[5 * layer][0].astype(F32)
        for term in terms[5 * layer + 1:5 * layer + 5]:
            total = total + term[0].astype(F32)
        sums.append(total.astype(BF))
    total = jnp.concatenate(sums, axis=1)
    row = lax.broadcasted_iota(jnp.int32, (256, 192), 0)
    source = lax.broadcasted_iota(jnp.int32, (256, 192), 1) - 6 * (row // 8)

    def pick(to, of):
        return jnp.where((row % 8 == to) & (source == of), 1.0, 0.0).astype(BF)

    main = jnp.where((row % 8 < 6) & (source == row % 8), 1.0, 0.0).astype(BF)
    out = mm(main, total[:, :MAIN])
    extra = [
        mm(pick(6, q), total[:, MAIN:MAIN + 128]) + mm(pick(7, q), total[:, MAIN + 128:]) for q in range(6)
    ]
    extra.append(jnp.zeros((256, 128), F32))
    out_ref[...] = (out + jnp.concatenate(extra, axis=1)).astype(BF)


def last_sum_kernel(x, out_ref):
    total = x[0].astype(F32)
    for m in range(1, 32):
        total = total + x[m].astype(F32)
    total = total * (1.0 / 256.0)
    out_ref[:, :MAIN] = total[:6, :]
    for q in range(6):
        out_ref[q:q + 1, MAIN:MAIN + 128] = total[6:7, 128 * q:128 * q + 128]
        out_ref[q:q + 1, MAIN + 128:] = total[7:8, 128 * q:128 * q + 128]


def whole(shape):
    return pl.BlockSpec(shape, lambda g: (0,) * len(shape))


def of_layer(array, layer):
    return array, pl.BlockSpec((1,) + array.shape[1:], lambda g: (layer, 0, 0))


def columns(array, first, count):
    return array, pl.BlockSpec((array.shape[0], count), lambda g: (0, first))


def block_zero(array):
    return array, pl.BlockSpec((1,) + array.shape[1:], lambda g: (0, 0, 0))


def after(array):
    return array, pl.BlockSpec(memory_space=pl.ANY)


def call(kernel, ins, outs, scratch=(), flops=5e9):
    ins = [a if isinstance(a, tuple) else (a, whole(a.shape)) for a in ins]
    return pl.pallas_call(
        kernel,
        grid=(1,),
        in_specs=[spec for _, spec in ins],
        out_specs=[whole(s) for s, _ in outs],
        out_shape=[jax.ShapeDtypeStruct(s, d) for s, d in outs],
        scratch_shapes=list(scratch),
        compiler_params=pltpu.CompilerParams(vmem_limit_bytes=VMEM),
        cost_estimate=pl.CostEstimate(flops=int(flops), bytes_accessed=10_000, transcendentals=0),
    )(*[a for a, _ in ins])


CORE_PAIRS = [(j, j ^ 1) for j in range(8)]


def add(a, b):
    return (a.astype(F32) + b.astype(F32)).astype(BF)


def reduce_rows(keep, send):
    first = lax.ppermute(send, "gy", CORE_PAIRS)
    got = [
        lax.ppermute(add(keep[s:s + 1], first[s:s + 1]), "gy", [(j, (j + 2 * s) % 8) for j in range(8)])
        for s in (1, 2, 3)
    ]
    return [keep, first, *got]


def per_device(cotangent, saved_codes, saved_scales, gains, w_qkv, w_out):
    to_rows, to_cols, from_cols, to_depth, to_home = [jnp.asarray(m, BF) for m in token_orders()]
    cot = cotangent.reshape(T, C)
    probs_shape = ((6, T, T), BF)
    tokens = ((T, C), BF)
    pairs = ((T, 2 * C), BF)
    terms = [((4, 192, C), BF), ((4, 192, C), BF)]

    first, *moving = call(
        centre_kernel,
        [saved_codes.reshape(3, T, C), jnp.transpose(saved_scales, (0, 4, 1, 2, 3)).reshape(9, 16, 16), cot, to_rows],
        [pairs] + [((32, 2 * C), BF)] * 8,
        [pltpu.VMEM(*pairs)],
    )
    x2 = lax.all_to_all(first.reshape(8, 32, 2 * C), "gx", 0, 0, tiled=True).reshape(T, 2 * C)
    moving = moving[:1] + [
        lax.ppermute(moving[step], "gy", [(j, j ^ step) for j in range(8)]) for step in range(1, 8)
    ]
    stream2, saved2 = call(
        column_kernel,
        [x2, gains, of_layer(w_qkv, 2), of_layer(w_out, 2), to_cols] + [after(m) for m in moving[1:]],
        [((2 * T, C), BF), ((T, 5 * C), BF)],
        [pltpu.VMEM(*probs_shape)],
    )
    got2 = lax.all_to_all(stream2.reshape(64, 8, C), ("gy", "gx"), 0, 0, tiled=True).reshape(2 * T, C)
    keep2, send2 = call(column_weight_kernel, [saved2, columns(x2, 1, C)], terms)
    saved1, probs1, x1 = call(
        row_forward_kernel,
        moving + [gains, of_layer(w_qkv, 1)],
        [((T, 5 * C), BF), probs_shape, pairs],
    )
    both, parts1, stream2 = call(
        row_backward_kernel,
        [x1, got2, saved1, probs1, gains, of_layer(w_qkv, 1), of_layer(w_out, 1), from_cols, to_depth],
        [pairs, ((T, 3 * C), BF), tokens],
    )
    x0 = lax.all_to_all(both.reshape(4, 64, 2 * C), "gz", 0, 0, tiled=True).reshape(T, 2 * C)
    keep1, send1 = call(row_weight_kernel, [columns(saved1, 0, 2 * C), parts1, stream2], terms)
    sums2 = reduce_rows(keep2, send2)
    sums1 = reduce_rows(keep1, send1)
    grad, keep0, send0 = call(
        depth_kernel,
        [x0, gains, of_layer(w_qkv, 0), of_layer(w_out, 0)] + [after(m) for m in sums2[2:]],
        [tokens] + terms,
        [pltpu.VMEM(*probs_shape)],
    )
    grad = lax.all_to_all(grad.reshape(32, 8, C), ("gz", "gy"), 0, 0, tiled=True).reshape(T, C)
    (rows,) = call(
        sum_kernel,
        [block_zero(m) for m in reduce_rows(keep0, send0) + sums1 + sums2],
        [((T, MAIN), BF)],
    )
    rows = lax.all_to_all(rows.reshape(32, 8, MAIN), ("gz", "gx"), 0, 0, tiled=True)
    (grad,) = call(home_kernel, [grad, to_home], [tokens])
    (weight_grads,) = call(last_sum_kernel, [rows], [((6, 3 * C), F32)])
    return grad.reshape(cotangent.shape), weight_grads


def solution(mesh):
    in_specs = (
        P("gz", "gy", "gx", None),
        P(None, "gz", "gy", "gx", None),
        P(None, "gz", "gy", "gx", None),
        P(),
        P(),
        P(),
    )
    out_specs = (P("gz", "gy", "gx", None), P(("gz", "gy", "gx"), None))
    return jax.shard_map(
        per_device, mesh=mesh, in_specs=in_specs, out_specs=out_specs, check_vma=False
    )
```

profile of v0, /device:TPU:1, one launch (start us, length us, event | category | flops | bytes accessed | tf_op | source)
XLA Modules:
  0.0 136.8 jit_solution(10142426962862353297)
XLA Ops:
  0.6 2.8 %shard_map.122 = (bf16[256,768]{1,0:T(8,128)(2,1)}, bf16[32,768]{1,0:T(8,128)(2,1)}, bf16[32,768]{1,0:T(8,128)(2,1)}, bf16[32,768]{1,0:T(8,128)(2,1)}, bf16[32,7...) custom-call(bf16[3,256,384]{2,1,0:T(8,128)(2,1)} %bitcast.24, ...), custom_call_target="tpu_custom_call" | custom-call | flops 5000000000 | bytes 10000 | tf_op jit(solution)/shard_map/pallas_call | solution.py:308
  3.5 6.4 %all-to-all-start = ((bf16[8,32,768]{2,1,0:T(8,128)(2,1)}), bf16[8,32,768]{2,1,0:T(8,128)(2,1)S(1)}, u32[]{:S(2)}, u32[]{:S(2)}) async-start(bf16[8,32,768]{2,1,0:T(8,128)(2,1)} %bitcast.18), calls=%async_computation | async-start | bytes 786432 | tf_op jit(solution)/shard_map/all_to_all | solution.py:350
  9.8 1.0 collective-permute-start
  10.8 1.2 collective-permute-start.1
  12.0 0.5 collective-permute-start.2
  12.5 2.7 %collective-permute-start.3 = (bf16[32,768]{1,0:T(8,128)(2,1)}, bf16[32,768]{1,0:T(8,128)(2,1)S(1)}, u32[]{:S(2)}, u32[]{:S(2)}) collective-permute-start(bf16[32,768]{1,0:T(8,128)(2,1)} %get-tuple-element.30), channel_id=1, source_target_pairs={{0,32},{8,40},{16,48},{24,56},{32,0},{40,8},{48,16},{56,24},{1,33}... | collective-permute-start | bytes 147464 | tf_op jit(solution)/shard_map/ppermute | solution.py:352
  15.3 0.6 collective-permute-start.4
  15.8 0.0 collective-permute-done.refs_1_.refs_0_
  15.8 2.5 %collective-permute-start.5 = (bf16[32,768]{1,0:T(8,128)(2,1)}, bf16[32,768]{1,0:T(8,128)(2,1)S(1)}, u32[]{:S(2)}, u32[]{:S(2)}) collective-permute-start(bf16[32,768]{1,0:T(8,128)(2,1)} %get-tuple-element.32), channel_id=1, source_target_pairs={{0,48},{8,56},{16,32},{24,40},{32,16},{40,24},{48,0},{56,8},{1,49}... | collective-permute-start | bytes 147464 | tf_op jit(solution)/shard_map/ppermute | solution.py:352
  18.3 0.0 collective-permute-done.1.refs_2_.refs_1_
  18.3 0.4 collective-permute-start.6
  18.7 0.0 collective-permute-done.2.refs_3_.refs_2_
  18.7 0.1 collective-permute-done.3.refs_4_.refs_3_
  18.8 2.1 %collective-permute-done.4.refs_5_.refs_4_ = bf16[32,768]{1,0:T(8,128)(2,1)S(1)} collective-permute-done((bf16[32,768]{1,0:T(8,128)(2,1)}, bf16[32,768]{1,0:T(8,128)(2,1)S(1)}, u32[]{:S(2)}, u32[]{:S(2)}) %collective-permute-start.4) | collective-permute-done | bytes 49184 | tf_op jit(solution)/shard_map/ppermute | solution.py:352
  20.9 1.0 collective-permute-done.5.refs_6_.refs_5_
  21.9 1.5 %collective-permute-done.6.refs_7_.refs_6_ = bf16[32,768]{1,0:T(8,128)(2,1)S(1)} collective-permute-done((bf16[32,768]{1,0:T(8,128)(2,1)}, bf16[32,768]{1,0:T(8,128)(2,1)S(1)}, u32[]{:S(2)}, u32[]{:S(2)}) %collective-permute-start.6) | collective-permute-done | bytes 49184 | tf_op jit(solution)/shard_map/ppermute | solution.py:352
  23.4 0.0 all-to-all-done
  23.5 0.6 copy-done.25
  24.0 0.1 copy-done.1
  24.2 6.4 %shard_map.124 = (bf16[512,384]{1,0:T(8,128)(2,1)}, bf16[256,1920]{1,0:T(8,128)(2,1)}) custom-call(bf16[256,768]{1,0:T(8,128)(2,1)} %bitcast.16, f32[3,384]{1,0:T(4,128)} %gains.5, bf16[3,384,1152]{2,1,0:T(8,128)(2,1)} %w_qkv.5, bf16[3,384,384]{2,1,0:T(8,128)(2,1)} %w_out.5, bf16[512,256]{1,0:T(8,128)(2,1)} %constant.11.clone.order, ...), custom_call_target="tpu_custom_call" | custom-call | flops 5000000000 | bytes 10000 | tf_op jit(solution)/shard_map/pallas_call | solution.py:308
  30.6 7.1 %all-to-all-start.1 = ((bf16[64,8,384]{2,1,0:T(8,128)(2,1)}), bf16[64,8,384]{2,1,0:T(8,128)(2,1)S(1)}, u32[]{:S(2)}, u32[]{:S(2)}) async-start(bf16[64,8,384]{2,1,0:T(8,128)(2,1)} %bitcast.22), calls=%async_computation.1 | async-start | bytes 786432 | tf_op jit(solution)/shard_map/all_to_all | solution.py:360
  37.7 3.8 %shard_map.126 = (bf16[4,192,384]{2,1,0:T(8,128)(2,1)}, bf16[4,192,384]{2,1,0:T(8,128)(2,1)}) custom-call(bf16[256,1920]{1,0:T(8,128)(2,1)} %get-tuple-element.40.saved, bf16[256,768]{1,0:T(8,128)(2,1)} %bitcast.17), custom_call_target="tpu_custom_call" | custom-call | flops 5000000000 | bytes 10000 | tf_op jit(solution)/shard_map/pallas_call | solution.py:308
  41.4 0.5 collective-permute-start.7
  41.9 4.5 %shard_map.123 = (bf16[256,1920]{1,0:T(8,128)(2,1)}, bf16[6,256,256]{2,1,0:T(8,128)(2,1)}, bf16[256,768]{1,0:T(8,128)(2,1)}) custom-call(bf16[32,768]{1,0:T(8,128)(2,1)} %get-tuple-element.26.refs_0_, bf16[32,768]{1,0:T(8,128)(2,1)} %copy-done.19, bf16[32,768]{1,0:T(8,128)(2,1)} %copy-done.20, bf16[32,768]{1,0:T(8,128)(2,1)} %copy-done.21, ...), custom_call_target="tpu_custom_call" | custom-call | flops 5000000000 | bytes 10000 | tf_op jit(solution)/shard_map/pallas_call | solution.py:308
  46.4 2.3 %all-to-all-done.1 = bf16[64,8,384]{2,1,0:T(8,128)(2,1)S(1)} async-done(((bf16[64,8,384]{2,1,0:T(8,128)(2,1)}), bf16[64,8,384]{2,1,0:T(8,128)(2,1)S(1)}, u32[]{:S(2)}, u32[]{:S(2)}) %all-to-all-start.1) | async-done | bytes 393248 | tf_op jit(solution)/shard_map/all_to_all | solution.py:360
  48.7 0.7 copy-done.3
  49.5 5.8 %shard_map.125 = (bf16[256,768]{1,0:T(8,128)(2,1)}, bf16[256,1152]{1,0:T(8,128)(2,1)}, bf16[256,384]{1,0:T(8,128)(2,1)}) custom-call(bf16[256,768]{1,0:T(8,128)(2,1)} %get-tuple-element.34.x, bf16[512,384]{1,0:T(8,128)(2,1)} %bitcast.21, bf16[256,1920]{1,0:T(8,128)(2,1)} %get-tuple-element.37.saved, bf16[6,256,256]{2,1,0:T(8,128)(2,1)} %get-tuple-element.38.probs, ...), custom_call_target="tpu_custom_call" | custom-call | flops 5000000000 | bytes 10000 | tf_op jit(solution)/shard_map/pallas_call | solution.py:308
  55.3 7.3 %all-to-all-start.2 = ((bf16[4,64,768]{2,1,0:T(8,128)(2,1)}), bf16[4,64,768]{2,1,0:T(8,128)(2,1)S(1)}, u32[]{:S(2)}, u32[]{:S(2)}) async-start(bf16[4,64,768]{2,1,0:T(8,128)(2,1)} %bitcast.20), calls=%async_computation.2 | async-start | bytes 786432 | tf_op jit(solution)/shard_map/all_to_all | solution.py:372
  62.6 0.0 collective-permute-done.7.refs_11_
  62.6 0.1 add_convert_fusion.6
  62.7 0.8 collective-permute-start.10
  63.4 0.3 collective-permute-start.9
  63.7 0.5 collective-permute-start.8
  64.2 3.7 %shard_map.129 = (bf16[4,192,384]{2,1,0:T(8,128)(2,1)}, bf16[4,192,384]{2,1,0:T(8,128)(2,1)}) custom-call(bf16[256,1920]{1,0:T(8,128)(2,1)} %get-tuple-element.37.saved, bf16[256,1152]{1,0:T(8,128)(2,1)} %get-tuple-element.46.parts, bf16[256,384]{1,0:T(8,128)(2,1)} %get-tuple-element.47.stream), custom_call_target="tpu_custom_call" | custom-call | flops 5000000000 | bytes 10000 | tf_op jit(solution)/shard_map/pallas_call | solution.py:308
  68.0 2.2 %collective-permute-start.15 = (bf16[4,192,384]{2,1,0:T(8,128)(2,1)}, bf16[4,192,384]{2,1,0:T(8,128)(2,1)S(1)}, u32[]{:S(2)}, u32[]{:S(2)}) collective-permute-start(bf16[4,192,384]{2,1,0:T(8,128)(2,1)} %get-tuple-element.49), channel_id=1, source_target_pairs={{0,8},{8,0},{16,24},{24,16},{32,40},{40,32},{48,56},{56,48},{1,9},... | collective-permute-start | bytes 1769480 | tf_op jit(solution)/shard_map/ppermute | solution.py:328
  70.2 0.0 collective-permute-done.10.refs_2_.refs_14_
  70.2 0.0 collective-permute-done.9.refs_1_.refs_13_
  70.2 3.1 %collective-permute-done.8.refs_0_.refs_12_ = bf16[1,192,384]{2,1,0:T(8,128)(2,1)S(1)} collective-permute-done((bf16[1,192,384]{2,1,0:T(8,128)(2,1)S(1)}, bf16[1,192,384]{2,1,0:T(8,128)(2,1)S(1)}, u32[]{:S(2)}, u32[]{:S(2)}) %collective-permute-start.8) | collective-permute-done | bytes 147488 | tf_op jit(solution)/shard_map/ppermute | solution.py:330
  73.3 1.3 all-to-all-done.2
  74.6 0.8 copy-done.2
  75.4 7.8 %shard_map.127 = (bf16[256,384]{1,0:T(8,128)(2,1)}, bf16[4,192,384]{2,1,0:T(8,128)(2,1)}, bf16[4,192,384]{2,1,0:T(8,128)(2,1)}) custom-call(bf16[256,768]{1,0:T(8,128)(2,1)} %bitcast.19, f32[3,384]{1,0:T(4,128)} %gains.5, bf16[3,384,1152]{2,1,0:T(8,128)(2,1)} %w_qkv.5, bf16[3,384,384]{2,1,0:T(8,128)(2,1)} %w_out.5, bf16[1,192,384]{2,1,0:T(8,128)(2,1)} %copy-done.12, ...), custom_call_target="tpu_custom_call" | custom-call | flops 5000000000 | bytes 10000 | tf_op jit(solution)/shard_map/pallas_call | solution.py:308
  83.2 1.6 %collective-permute-start.11 = (bf16[4,192,384]{2,1,0:T(8,128)(2,1)}, bf16[4,192,384]{2,1,0:T(8,128)(2,1)S(1)}, u32[]{:S(2)}, u32[]{:S(2)}) collective-permute-start(bf16[4,192,384]{2,1,0:T(8,128)(2,1)} %get-tuple-element.45), channel_id=1, source_target_pairs={{0,8},{8,0},{16,24},{24,16},{32,40},{40,32},{48,56},{56,48},{1,9},... | collective-permute-start | bytes 1769480 | tf_op jit(solution)/shard_map/ppermute | solution.py:328
  84.8 0.0 collective-permute-done.15.refs_6_
  84.8 0.1 add_convert_fusion
  84.9 1.4 collective-permute-start.18
  86.3 0.7 collective-permute-start.17
  87.0 0.4 collective-permute-start.16
  87.4 0.0 collective-permute-done.11.refs_1_
  87.4 1.4 %add_convert_fusion.3 = (bf16[1,192,384]{2,1,0:T(8,128)(2,1)S(1)}, bf16[1,192,384]{2,1,0:T(8,128)(2,1)S(1)}, bf16[1,192,384]{2,1,0:T(8,128)(2,1)S(1)}) fusion(bf16[4,192,384]{2,1,0:T(8,128)(2,1)S(1)} %collective-permute-done.11.refs_1_, bf16[4,192,384]{2,1,0:T(8,128)(2,1)} %get-tuple-element.44.refs_0_), kind=kLoop, calls=%fused_computation.3 | loop fusion | flops 884736 | bytes 1327104 | tf_op jit(solution)/shard_map/convert_element_type | solution.py:324
  88.8 2.3 %collective-permute-start.14 = (bf16[1,192,384]{2,1,0:T(8,128)(2,1)S(1)}, bf16[1,192,384]{2,1,0:T(8,128)(2,1)S(1)}, u32[]{:S(2)}, u32[]{:S(2)}) collective-permute-start(bf16[1,192,384]{2,1,0:T(8,128)(2,1)S(1)} %get-tuple-element.53), channel_id=1, source_target_pairs={{0,48},{8,56},{16,0},{24,8},{32,16},{40,24},{48,32},{56,40},{1,49}... | collective-permute-start | bytes 442376 | tf_op jit(solution)/shard_map/ppermute | solution.py:330
  91.1 1.1 collective-permute-start.13
  92.2 0.2 collective-permute-start.12
  92.4 8.3 %all-to-all-start.3 = ((bf16[32,8,384]{2,1,0:T(8,128)(2,1)}), bf16[32,8,384]{2,1,0:T(8,128)(2,1)S(1)}, u32[]{:S(2)}, u32[]{:S(2)}) async-start(bf16[32,8,384]{2,1,0:T(8,128)(2,1)} %bitcast.10), calls=%async_computation.3 | async-start | bytes 393216 | tf_op jit(solution)/shard_map/all_to_all | solution.py:382
  100.8 0.0 collective-permute-done.14.refs_4_
  100.8 0.0 collective-permute-done.13.refs_3_
  100.8 2.1 %collective-permute-done.12.refs_2_ = bf16[1,192,384]{2,1,0:T(8,128)(2,1)S(1)} collective-permute-done((bf16[1,192,384]{2,1,0:T(8,128)(2,1)S(1)}, bf16[1,192,384]{2,1,0:T(8,128)(2,1)S(1)}, u32[]{:S(2)}, u32[]{:S(2)}) %collective-permute-start.12) | collective-permute-done | bytes 147488 | tf_op jit(solution)/shard_map/ppermute | solution.py:330
  103.0 0.7 copy-done.18
  103.7 3.3 %shard_map.130 = bf16[256,896]{1,0:T(8,128)(2,1)} custom-call(bf16[4,192,384]{2,1,0:T(8,128)(2,1)} %get-tuple-element.44.refs_0_, bf16[4,192,384]{2,1,0:T(8,128)(2,1)} %copy-done.8, bf16[1,192,384]{2,1,0:T(8,128)(2,1)} %copy-done.18, bf16[1,192,384]{2,1,0:T(8,128)(2,1)} %copy-done.17, bf16[1,192,384]{2,1,0:T(8,128)(2,1)} %copy-done.16, ...), custom_call_target="tpu_custom_call" | custom-call | flops 5000000000 | bytes 10000 | tf_op jit(solution)/shard_map/pallas_call | solution.py:308
  107.0 6.4 %all-to-all-done.3 = bf16[32,8,384]{2,1,0:T(8,128)(2,1)S(1)} async-done(((bf16[32,8,384]{2,1,0:T(8,128)(2,1)}), bf16[32,8,384]{2,1,0:T(8,128)(2,1)S(1)}, u32[]{:S(2)}, u32[]{:S(2)}) %all-to-all-start.3) | async-done | bytes 196640 | tf_op jit(solution)/shard_map/all_to_all | solution.py:382
  113.3 5.4 %all-to-all-start.4 = ((bf16[32,8,896]{2,1,0:T(8,128)(2,1)}), bf16[32,8,896]{2,1,0:T(8,128)(2,1)S(1)}, u32[]{:S(2)}, u32[]{:S(2)}) async-start(bf16[32,8,896]{2,1,0:T(8,128)(2,1)} %bitcast.15), calls=%async_computation.4 | async-start | bytes 917504 | tf_op jit(solution)/shard_map/all_to_all | solution.py:388
  118.7 1.9 %shard_map.128 = bf16[256,384]{1,0:T(8,128)(2,1)} custom-call(bf16[256,384]{1,0:T(8,128)(2,1)} %bitcast.23, bf16[256,256]{1,0:T(8,128)(2,1)} %constant.14.clone.order), custom_call_target="tpu_custom_call" | custom-call | flops 5000000000 | bytes 10000 | tf_op jit(solution)/shard_map/pallas_call | solution.py:308
  120.6 13.6 %all-to-all-done.4.x = bf16[32,8,896]{2,1,0:T(8,128)(2,1)S(1)} async-done(((bf16[32,8,896]{2,1,0:T(8,128)(2,1)}), bf16[32,8,896]{2,1,0:T(8,128)(2,1)S(1)}, u32[]{:S(2)}, u32[]{:S(2)}) %all-to-all-start.4) | async-done | bytes 458784 | tf_op jit(solution)/shard_map/all_to_all | solution.py:388
  134.3 0.8 copy-done
  135.1 1.7 %shard_map.131 = f32[6,1152]{1,0:T(8,128)} custom-call(bf16[32,8,896]{2,1,0:T(8,128)(2,1)} %copy-done), custom_call_target="tpu_custom_call" | custom-call | flops 5000000000 | bytes 10000 | tf_op jit(solution)/shard_map/pallas_call | solution.py:308
  (49 shorter events, 0.1 us)
Async XLA Ops:
  3.5 20.0 %all-to-all-start = ((bf16[8,32,768]{2,1,0:T(8,128)(2,1)}), bf16[8,32,768]{2,1,0:T(8,128)(2,1)S(1)}, u32[]{:S(2)}, u32[]{:S(2)}) async-start(bf16[8,32,768]{2,1,0:T(8,128)(2,1)} %bitcast.18), calls=%async_computation | async-start | bytes 786432 | tf_op jit(solution)/shard_map/all_to_all | solution.py:350
  9.8 6.0 %collective-permute-start = (bf16[32,768]{1,0:T(8,128)(2,1)}, bf16[32,768]{1,0:T(8,128)(2,1)S(1)}, u32[]{:S(2)}, u32[]{:S(2)}) collective-permute-start(bf16[32,768]{1,0:T(8,128)(2,1)} %get-tuple-element.27), channel_id=1, source_target_pairs={{0,8},{8,0},{16,24},{24,16},{32,40},{40,32},{48,56},{56,48},{1,9},... | collective-permute-start | bytes 147464 | tf_op jit(solution)/shard_map/ppermute | solution.py:352
  10.8 7.5 %collective-permute-start.1 = (bf16[32,768]{1,0:T(8,128)(2,1)}, bf16[32,768]{1,0:T(8,128)(2,1)S(1)}, u32[]{:S(2)}, u32[]{:S(2)}) collective-permute-start(bf16[32,768]{1,0:T(8,128)(2,1)} %get-tuple-element.28), channel_id=1, source_target_pairs={{0,16},{8,24},{16,0},{24,8},{32,48},{40,56},{48,32},{56,40},{1,17}... | collective-permute-start | bytes 147464 | tf_op jit(solution)/shard_map/ppermute | solution.py:352
  12.0 6.7 %collective-permute-start.2 = (bf16[32,768]{1,0:T(8,128)(2,1)}, bf16[32,768]{1,0:T(8,128)(2,1)S(1)}, u32[]{:S(2)}, u32[]{:S(2)}) collective-permute-start(bf16[32,768]{1,0:T(8,128)(2,1)} %get-tuple-element.29), channel_id=1, source_target_pairs={{0,24},{8,16},{16,8},{24,0},{32,56},{40,48},{48,40},{56,32},{1,25}... | collective-permute-start | bytes 147464 | tf_op jit(solution)/shard_map/ppermute | solution.py:352
  12.5 6.3 %collective-permute-start.3 = (bf16[32,768]{1,0:T(8,128)(2,1)}, bf16[32,768]{1,0:T(8,128)(2,1)S(1)}, u32[]{:S(2)}, u32[]{:S(2)}) collective-permute-start(bf16[32,768]{1,0:T(8,128)(2,1)} %get-tuple-element.30), channel_id=1, source_target_pairs={{0,32},{8,40},{16,48},{24,56},{32,0},{40,8},{48,16},{56,24},{1,33}... | collective-permute-start | bytes 147464 | tf_op jit(solution)/shard_map/ppermute | solution.py:352
  15.3 5.6 %collective-permute-start.4 = (bf16[32,768]{1,0:T(8,128)(2,1)}, bf16[32,768]{1,0:T(8,128)(2,1)S(1)}, u32[]{:S(2)}, u32[]{:S(2)}) collective-permute-start(bf16[32,768]{1,0:T(8,128)(2,1)} %get-tuple-element.31), channel_id=1, source_target_pairs={{0,40},{8,32},{16,56},{24,48},{32,8},{40,0},{48,24},{56,16},{1,41}... | collective-permute-start | bytes 147464 | tf_op jit(solution)/shard_map/ppermute | solution.py:352
  15.8 7.6 %copy-start.19 = (bf16[32,768]{1,0:T(8,128)(2,1)}, bf16[32,768]{1,0:T(8,128)(2,1)S(1)}, u32[]{:S(2)}) copy-start(bf16[32,768]{1,0:T(8,128)(2,1)S(1)} %collective-permute-done.refs_1_.refs_0_) | copy-start | bytes 147460
  15.8 6.1 %collective-permute-start.5 = (bf16[32,768]{1,0:T(8,128)(2,1)}, bf16[32,768]{1,0:T(8,128)(2,1)S(1)}, u32[]{:S(2)}, u32[]{:S(2)}) collective-permute-start(bf16[32,768]{1,0:T(8,128)(2,1)} %get-tuple-element.32), channel_id=1, source_target_pairs={{0,48},{8,56},{16,32},{24,40},{32,16},{40,24},{48,0},{56,8},{1,49}... | collective-permute-start | bytes 147464 | tf_op jit(solution)/shard_map/ppermute | solution.py:352
  18.3 5.1 %copy-start.20 = (bf16[32,768]{1,0:T(8,128)(2,1)}, bf16[32,768]{1,0:T(8,128)(2,1)S(1)}, u32[]{:S(2)}) copy-start(bf16[32,768]{1,0:T(8,128)(2,1)S(1)} %collective-permute-done.1.refs_2_.refs_1_) | copy-start | bytes 147460
  18.3 5.1 %collective-permute-start.6 = (bf16[32,768]{1,0:T(8,128)(2,1)}, bf16[32,768]{1,0:T(8,128)(2,1)S(1)}, u32[]{:S(2)}, u32[]{:S(2)}) collective-permute-start(bf16[32,768]{1,0:T(8,128)(2,1)} %get-tuple-element.33), channel_id=1, source_target_pairs={{0,56},{8,48},{16,40},{24,32},{32,24},{40,16},{48,8},{56,0},{1,57}... | collective-permute-start | bytes 147464 | tf_op jit(solution)/shard_map/ppermute | solution.py:352
  18.7 4.7 %copy-start.21 = (bf16[32,768]{1,0:T(8,128)(2,1)}, bf16[32,768]{1,0:T(8,128)(2,1)S(1)}, u32[]{:S(2)}) copy-start(bf16[32,768]{1,0:T(8,128)(2,1)S(1)} %collective-permute-done.2.refs_3_.refs_2_) | copy-start | bytes 147460
  18.8 4.6 %copy-start.22 = (bf16[32,768]{1,0:T(8,128)(2,1)}, bf16[32,768]{1,0:T(8,128)(2,1)S(1)}, u32[]{:S(2)}) copy-start(bf16[32,768]{1,0:T(8,128)(2,1)S(1)} %collective-permute-done.3.refs_4_.refs_3_) | copy-start | bytes 147460
  20.9 2.6 %copy-start.23 = (bf16[32,768]{1,0:T(8,128)(2,1)}, bf16[32,768]{1,0:T(8,128)(2,1)S(1)}, u32[]{:S(2)}) copy-start(bf16[32,768]{1,0:T(8,128)(2,1)S(1)} %collective-permute-done.4.refs_5_.refs_4_) | copy-start | bytes 147460
  21.9 1.6 %copy-start.24 = (bf16[32,768]{1,0:T(8,128)(2,1)}, bf16[32,768]{1,0:T(8,128)(2,1)S(1)}, u32[]{:S(2)}) copy-start(bf16[32,768]{1,0:T(8,128)(2,1)S(1)} %collective-permute-done.5.refs_6_.refs_5_) | copy-start | bytes 147460
  23.4 0.6 copy-start.25
  23.4 0.8 copy-start.1
  30.6 18.1 %all-to-all-start.1 = ((bf16[64,8,384]{2,1,0:T(8,128)(2,1)}), bf16[64,8,384]{2,1,0:T(8,128)(2,1)S(1)}, u32[]{:S(2)}, u32[]{:S(2)}) async-start(bf16[64,8,384]{2,1,0:T(8,128)(2,1)} %bitcast.22), calls=%async_computation.1 | async-start | bytes 786432 | tf_op jit(solution)/shard_map/all_to_all | solution.py:360
  41.4 21.1 %collective-permute-start.7 = (bf16[4,192,384]{2,1,0:T(8,128)(2,1)}, bf16[4,192,384]{2,1,0:T(8,128)(2,1)S(1)}, u32[]{:S(2)}, u32[]{:S(2)}) collective-permute-start(bf16[4,192,384]{2,1,0:T(8,128)(2,1)} %get-tuple-element.42), channel_id=1, source_target_pairs={{0,8},{8,0},{16,24},{24,16},{32,40},{40,32},{48,56},{56,48},{1,9},... | collective-permute-start | bytes 1769480 | tf_op jit(solution)/shard_map/ppermute | solution.py:328
  48.7 0.7 copy-start.3
  49.5 13.1 %copy-start.4 = (bf16[4,192,384]{2,1,0:T(8,128)(2,1)S(1)}, bf16[4,192,384]{2,1,0:T(8,128)(2,1)}, u32[]{:S(2)}) copy-start(bf16[4,192,384]{2,1,0:T(8,128)(2,1)} %get-tuple-element.41.refs_10_) | copy-start | bytes 1769476
  55.3 19.3 %all-to-all-start.2 = ((bf16[4,64,768]{2,1,0:T(8,128)(2,1)}), bf16[4,64,768]{2,1,0:T(8,128)(2,1)S(1)}, u32[]{:S(2)}, u32[]{:S(2)}) async-start(bf16[4,64,768]{2,1,0:T(8,128)(2,1)} %bitcast.20), calls=%async_computation.2 | async-start | bytes 786432 | tf_op jit(solution)/shard_map/all_to_all | solution.py:372
  62.6 5.4 %copy-start.5 = (bf16[4,192,384]{2,1,0:T(8,128)(2,1)}, bf16[4,192,384]{2,1,0:T(8,128)(2,1)S(1)}, u32[]{:S(2)}) copy-start(bf16[4,192,384]{2,1,0:T(8,128)(2,1)S(1)} %collective-permute-done.7.refs_11_) | copy-start | bytes 1769476
  62.7 7.5 %collective-permute-start.10 = (bf16[1,192,384]{2,1,0:T(8,128)(2,1)S(1)}, bf16[1,192,384]{2,1,0:T(8,128)(2,1)S(1)}, u32[]{:S(2)}, u32[]{:S(2)}) collective-permute-start(bf16[1,192,384]{2,1,0:T(8,128)(2,1)S(1)} %get-tuple-element.56), channel_id=1, source_target_pairs={{0,48},{8,56},{16,0},{24,8},{32,16},{40,24},{48,32},{56,40},{1,49}... | collective-permute-start | bytes 442376 | tf_op jit(solution)/shard_map/ppermute | solution.py:330
  63.4 6.7 %collective-permute-start.9 = (bf16[1,192,384]{2,1,0:T(8,128)(2,1)S(1)}, bf16[1,192,384]{2,1,0:T(8,128)(2,1)S(1)}, u32[]{:S(2)}, u32[]{:S(2)}) collective-permute-start(bf16[1,192,384]{2,1,0:T(8,128)(2,1)S(1)} %get-tuple-element.57), channel_id=1, source_target_pairs={{0,32},{8,40},{16,48},{24,56},{32,0},{40,8},{48,16},{56,24},{1,33}... | collective-permute-start | bytes 442376 | tf_op jit(solution)/shard_map/ppermute | solution.py:330
  63.7 9.6 %collective-permute-start.8 = (bf16[1,192,384]{2,1,0:T(8,128)(2,1)S(1)}, bf16[1,192,384]{2,1,0:T(8,128)(2,1)S(1)}, u32[]{:S(2)}, u32[]{:S(2)}) collective-permute-start(bf16[1,192,384]{2,1,0:T(8,128)(2,1)S(1)} %get-tuple-element.58), channel_id=1, source_target_pairs={{0,16},{8,24},{16,32},{24,40},{32,48},{40,56},{48,0},{56,8},{1,17}... | collective-permute-start | bytes 442376 | tf_op jit(solution)/shard_map/ppermute | solution.py:330
  68.0 16.8 %collective-permute-start.15 = (bf16[4,192,384]{2,1,0:T(8,128)(2,1)}, bf16[4,192,384]{2,1,0:T(8,128)(2,1)S(1)}, u32[]{:S(2)}, u32[]{:S(2)}) collective-permute-start(bf16[4,192,384]{2,1,0:T(8,128)(2,1)} %get-tuple-element.49), channel_id=1, source_target_pairs={{0,8},{8,0},{16,24},{24,16},{32,40},{40,32},{48,56},{56,48},{1,9},... | collective-permute-start | bytes 1769480 | tf_op jit(solution)/shard_map/ppermute | solution.py:328
  70.2 4.4 %copy-start.10 = (bf16[1,192,384]{2,1,0:T(8,128)(2,1)}, bf16[1,192,384]{2,1,0:T(8,128)(2,1)S(1)}, u32[]{:S(2)}) copy-start(bf16[1,192,384]{2,1,0:T(8,128)(2,1)S(1)} %collective-permute-done.10.refs_2_.refs_14_) | copy-start | bytes 442372
  70.2 4.4 %copy-start.11 = (bf16[1,192,384]{2,1,0:T(8,128)(2,1)}, bf16[1,192,384]{2,1,0:T(8,128)(2,1)S(1)}, u32[]{:S(2)}) copy-start(bf16[1,192,384]{2,1,0:T(8,128)(2,1)S(1)} %collective-permute-done.9.refs_1_.refs_13_) | copy-start | bytes 442372
  73.3 1.3 copy-start.12
  74.6 0.8 copy-start.2
  75.4 9.4 %copy-start.6 = (bf16[4,192,384]{2,1,0:T(8,128)(2,1)S(1)}, bf16[4,192,384]{2,1,0:T(8,128)(2,1)}, u32[]{:S(2)}) copy-start(bf16[4,192,384]{2,1,0:T(8,128)(2,1)} %get-tuple-element.48.refs_5_) | copy-start | bytes 1769476
  83.2 4.2 %collective-permute-start.11 = (bf16[4,192,384]{2,1,0:T(8,128)(2,1)}, bf16[4,192,384]{2,1,0:T(8,128)(2,1)S(1)}, u32[]{:S(2)}, u32[]{:S(2)}) collective-permute-start(bf16[4,192,384]{2,1,0:T(8,128)(2,1)} %get-tuple-element.45), channel_id=1, source_target_pairs={{0,8},{8,0},{16,24},{24,16},{32,40},{40,32},{48,56},{56,48},{1,9},... | collective-permute-start | bytes 1769480 | tf_op jit(solution)/shard_map/ppermute | solution.py:328
  84.8 18.1 %copy-start.7 = (bf16[4,192,384]{2,1,0:T(8,128)(2,1)}, bf16[4,192,384]{2,1,0:T(8,128)(2,1)S(1)}, u32[]{:S(2)}) copy-start(bf16[4,192,384]{2,1,0:T(8,128)(2,1)S(1)} %collective-permute-done.15.refs_6_) | copy-start | bytes 1769476
  84.9 7.3 %collective-permute-start.18 = (bf16[1,192,384]{2,1,0:T(8,128)(2,1)S(1)}, bf16[1,192,384]{2,1,0:T(8,128)(2,1)S(1)}, u32[]{:S(2)}, u32[]{:S(2)}) collective-permute-start(bf16[1,192,384]{2,1,0:T(8,128)(2,1)S(1)} %get-tuple-element.50), channel_id=1, source_target_pairs={{0,48},{8,56},{16,0},{24,8},{32,16},{40,24},{48,32},{56,40},{1,49}... | collective-permute-start | bytes 442376 | tf_op jit(solution)/shard_map/ppermute | solution.py:330
  86.3 14.5 %collective-permute-start.17 = (bf16[1,192,384]{2,1,0:T(8,128)(2,1)S(1)}, bf16[1,192,384]{2,1,0:T(8,128)(2,1)S(1)}, u32[]{:S(2)}, u32[]{:S(2)}) collective-permute-start(bf16[1,192,384]{2,1,0:T(8,128)(2,1)S(1)} %get-tuple-element.51), channel_id=1, source_target_pairs={{0,32},{8,40},{16,48},{24,56},{32,0},{40,8},{48,16},{56,24},{1,33}... | collective-permute-start | bytes 442376 | tf_op jit(solution)/shard_map/ppermute | solution.py:330
  87.0 13.8 %collective-permute-start.16 = (bf16[1,192,384]{2,1,0:T(8,128)(2,1)S(1)}, bf16[1,192,384]{2,1,0:T(8,128)(2,1)S(1)}, u32[]{:S(2)}, u32[]{:S(2)}) collective-permute-start(bf16[1,192,384]{2,1,0:T(8,128)(2,1)S(1)} %get-tuple-element.52), channel_id=1, source_target_pairs={{0,16},{8,24},{16,32},{24,40},{32,48},{40,56},{48,0},{56,8},{1,17}... | collective-permute-start | bytes 442376 | tf_op jit(solution)/shard_map/ppermute | solution.py:330
  87.4 15.6 %copy-start.8 = (bf16[4,192,384]{2,1,0:T(8,128)(2,1)}, bf16[4,192,384]{2,1,0:T(8,128)(2,1)S(1)}, u32[]{:S(2)}) copy-start(bf16[4,192,384]{2,1,0:T(8,128)(2,1)S(1)} %collective-permute-done.11.refs_1_) | copy-start | bytes 1769476
  88.8 12.0 %collective-permute-start.14 = (bf16[1,192,384]{2,1,0:T(8,128)(2,1)S(1)}, bf16[1,192,384]{2,1,0:T(8,128)(2,1)S(1)}, u32[]{:S(2)}, u32[]{:S(2)}) collective-permute-start(bf16[1,192,384]{2,1,0:T(8,128)(2,1)S(1)} %get-tuple-element.53), channel_id=1, source_target_pairs={{0,48},{8,56},{16,0},{24,8},{32,16},{40,24},{48,32},{56,40},{1,49}... | collective-permute-start | bytes 442376 | tf_op jit(solution)/shard_map/ppermute | solution.py:330
  91.1 9.7 %collective-permute-start.13 = (bf16[1,192,384]{2,1,0:T(8,128)(2,1)S(1)}, bf16[1,192,384]{2,1,0:T(8,128)(2,1)S(1)}, u32[]{:S(2)}, u32[]{:S(2)}) collective-permute-start(bf16[1,192,384]{2,1,0:T(8,128)(2,1)S(1)} %get-tuple-element.54), channel_id=1, source_target_pairs={{0,32},{8,40},{16,48},{24,56},{32,0},{40,8},{48,16},{56,24},{1,33}... | collective-permute-start | bytes 442376 | tf_op jit(solution)/shard_map/ppermute | solution.py:330
  92.2 10.8 %copy-start.13 = (bf16[1,192,384]{2,1,0:T(8,128)(2,1)}, bf16[1,192,384]{2,1,0:T(8,128)(2,1)S(1)}, u32[]{:S(2)}) copy-start(bf16[1,192,384]{2,1,0:T(8,128)(2,1)S(1)} %collective-permute-done.18.refs_9_) | copy-start | bytes 442372
  92.2 10.7 %collective-permute-start.12 = (bf16[1,192,384]{2,1,0:T(8,128)(2,1)S(1)}, bf16[1,192,384]{2,1,0:T(8,128)(2,1)S(1)}, u32[]{:S(2)}, u32[]{:S(2)}) collective-permute-start(bf16[1,192,384]{2,1,0:T(8,128)(2,1)S(1)} %get-tuple-element.55), channel_id=1, source_target_pairs={{0,16},{8,24},{16,32},{24,40},{32,48},{40,56},{48,0},{56,8},{1,17}... | collective-permute-start | bytes 442376 | tf_op jit(solution)/shard_map/ppermute | solution.py:330
  92.4 20.9 %all-to-all-start.3 = ((bf16[32,8,384]{2,1,0:T(8,128)(2,1)}), bf16[32,8,384]{2,1,0:T(8,128)(2,1)S(1)}, u32[]{:S(2)}, u32[]{:S(2)}) async-start(bf16[32,8,384]{2,1,0:T(8,128)(2,1)} %bitcast.10), calls=%async_computation.3 | async-start | bytes 393216 | tf_op jit(solution)/shard_map/all_to_all | solution.py:382
  100.8 2.2 %copy-start.14 = (bf16[1,192,384]{2,1,0:T(8,128)(2,1)}, bf16[1,192,384]{2,1,0:T(8,128)(2,1)S(1)}, u32[]{:S(2)}) copy-start(bf16[1,192,384]{2,1,0:T(8,128)(2,1)S(1)} %collective-permute-done.17.refs_8_) | copy-start | bytes 442372
  100.8 2.2 %copy-start.15 = (bf16[1,192,384]{2,1,0:T(8,128)(2,1)}, bf16[1,192,384]{2,1,0:T(8,128)(2,1)S(1)}, u32[]{:S(2)}) copy-start(bf16[1,192,384]{2,1,0:T(8,128)(2,1)S(1)} %collective-permute-done.16.refs_7_) | copy-start | bytes 442372
  100.8 2.2 %copy-start.16 = (bf16[1,192,384]{2,1,0:T(8,128)(2,1)}, bf16[1,192,384]{2,1,0:T(8,128)(2,1)S(1)}, u32[]{:S(2)}) copy-start(bf16[1,192,384]{2,1,0:T(8,128)(2,1)S(1)} %collective-permute-done.14.refs_4_) | copy-start | bytes 442372
  100.8 2.2 %copy-start.17 = (bf16[1,192,384]{2,1,0:T(8,128)(2,1)}, bf16[1,192,384]{2,1,0:T(8,128)(2,1)S(1)}, u32[]{:S(2)}) copy-start(bf16[1,192,384]{2,1,0:T(8,128)(2,1)S(1)} %collective-permute-done.13.refs_3_) | copy-start | bytes 442372
  103.0 0.7 copy-start.18
  113.3 5.4 %copy-start.9 = (bf16[32,8,384]{2,1,0:T(8,128)(2,1)}, bf16[32,8,384]{2,1,0:T(8,128)(2,1)S(1)}, u32[]{:S(2)}) copy-start(bf16[32,8,384]{2,1,0:T(8,128)(2,1)S(1)} %all-to-all-done.3) | copy-start | bytes 589828
  113.3 20.9 %all-to-all-start.4 = ((bf16[32,8,896]{2,1,0:T(8,128)(2,1)}), bf16[32,8,896]{2,1,0:T(8,128)(2,1)S(1)}, u32[]{:S(2)}, u32[]{:S(2)}) async-start(bf16[32,8,896]{2,1,0:T(8,128)(2,1)} %bitcast.15), calls=%async_computation.4 | async-start | bytes 917504 | tf_op jit(solution)/shard_map/all_to_all | solution.py:388
  134.3 0.8 copy-start
where the time goes:
time: 138 us; the launch traced here: 137 us
  starting transfers between devices  55.2 us (40%)
  Pallas kernels  41.7 us (30%)
  waiting for transfers between devices  33.6 us (24%)
  local copies, waits for them, and re-layouts  3.76 us (3%)
  other arithmetic  1.59 us (1%)
    pallas_call x10, Pallas kernels, call(): pl.pallas_call(kernel, grid=(1,), in_specs=[spec for _, spec in ins], out...  41.7 us
    all_to_all x1, waiting for transfers between devices, per_device(): lax.all_to_all(rows.reshape(32, 8, MAIN), ('gz', 'gx'), 0, 0, tiled=True)  13.6 us
    ppermute x7, starting transfers between devices, per_device(): lax.ppermute(moving[step], 'gy', [(j, j ^ step) for j in range(8)])  8.89 us
    all_to_all x1, starting transfers between devices, per_device(): lax.all_to_all(grad.reshape(32, 8, C), ('gz', 'gy'), 0, 0, tiled=True)  8.35 us
    ppermute x9, starting transfers between devices, reduce_rows(): lax.ppermute(add(keep[s:s + 1], first[s:s + 1]), 'gy', [(j, (j + 2 * s) %...  7.6 us
    all_to_all x1, starting transfers between devices, per_device(): lax.all_to_all(both.reshape(4, 64, 2 * C), 'gz', 0, 0, tiled=True)  7.29 us
    all_to_all x1, starting transfers between devices, per_device(): lax.all_to_all(stream2.reshape(64, 8, C), ('gy', 'gx'), 0, 0, tiled=True)  7.06 us
    all_to_all x1, starting transfers between devices, per_device(): lax.all_to_all(first.reshape(8, 32, 2 * C), 'gx', 0, 0, tiled=True)  6.37 us
  transfers between devices with their start and end apart: 24, of which 10 were waited for; matrix products, arithmetic and copies ran while one was open for 1% of the time, Pallas kernels for 22%

commit v1 on v0

--- a/solution.py
+++ b/solution.py
@@ -27,10 +27,12 @@
     to_rows = ((n % 32) // 2) * 16 + 2 * (n // 32) + n % 2
     j, i, r, c = n // 32, (n // 4) % 8, (n // 2) % 2, n % 2
     cols = i * 32 + r * 16 + 2 * j + c
-    to_cols = np.zeros((2 * T, T), np.float32)
-    to_cols[8 * (n // 4) + n % 4, cols] = 1.0
-    from_cols = np.zeros((T, 2 * T), np.float32)
-    from_cols[n, 8 * (n // 4) + n % 4] = 1.0
+    to_cols = np.zeros((4 * T, T), np.float32)
+    from_cols = np.zeros((T, 4 * T), np.float32)
+    for g in range(3):
+        at = 16 * (n // 4) + 4 * g + n % 4
+        to_cols[at, cols] = 1.0
+        from_cols[n, at] = 1.0
     z, j, r, c = n // 64, (n // 8) % 8, (n // 2) % 4, n % 2
     to_depth = j * 32 + z * 8 + r * 2 + c
     z, r, j, c = n // 64, (n // 16) % 4, (n // 2) % 8, n % 2
@@ -157,32 +159,32 @@
                 send_ref[at] = block
 
 
-def place(index, count):
-    return pl.ds(pl.multiple_of(count * index, count), count)
-
-
-def centre_kernel(codes, scales, cot, order, first_ref, *refs):
+def centred(codes, scales):
     token = lax.broadcasted_iota(jnp.int32, (T, 16), 0)
     lane = lax.broadcasted_iota(jnp.int32, (T, 16), 1)
     row_of = jnp.where(token // 16 == lane, 1.0, 0.0).astype(BF)
     col_of = jnp.where(token % 16 == lane, 1.0, 0.0).astype(F32)
     ones = jnp.ones((16, 128), BF)
-
-    def centred(layer):
-        blocks = []
-        for b in range(3):
-            own = (mm(row_of, scales[3 * layer + b]) * col_of).astype(BF)
-            blocks.append(codes[layer, :, 128 * b:128 * b + 128].astype(F32) * mm(own, ones))
-        h = jnp.concatenate(blocks, axis=1)
-        return (h - jnp.mean(h, axis=-1, keepdims=True)).astype(BF)
-
-    first_ref[:, :C] = centred(2)
-    first_ref[:, C:] = cot[...]
-    both = jnp.concatenate([centred(1), centred(0)], axis=1)
-    refs[-1][...] = mm(order[...], both).astype(BF)
-    me = lax.axis_index("gy")
-    for step in range(8):
-        refs[step][...] = refs[-1][place(me ^ step, 32), :]
+    blocks = []
+    for b in range(3):
+        own = (mm(row_of, scales[b]) * col_of).astype(BF)
+        blocks.append(codes[:, 128 * b:128 * b + 128].astype(F32) * mm(own, ones))
+    h = jnp.concatenate(blocks, axis=1)
+    return (h - jnp.mean(h, axis=-1, keepdims=True)).astype(BF)
+
+
+def first_kernel(codes, scales, cot, out_ref):
+    out_ref[:, :C] = centred(codes[0], scales)
+    out_ref[:, C:] = cot[...]
+
+
+def second_kernel(codes, scales, order, out_ref):
+    both = jnp.concatenate([centred(codes[1], scales[3:]), centred(codes[0], scales[:3])], axis=1)
+    out_ref[...] = mm(order[...], both).astype(BF)
+
+
+def message_group():
+    return lax.broadcasted_iota(jnp.int32, (4 * T, 128), 0) % 16 // 4
 
 
 def column_kernel(x, gains, w_qkv, w_out, order, *refs):
@@ -192,25 +194,28 @@
     normed, queries, keys, values, attended = forward(2, y, gain, wq, probs_ref)
     parts = backward_attention(stream, wo, queries, keys, values, probs_ref)
     new = backward_input(y, stream, gain, wq, parts)
-    stream_ref[...] = mm(order[...], new).astype(BF)
+    wide = mm(order[...], new)
+    group = message_group()
+    stream_ref[...] = jnp.where(
+        group == 0, wide[:, :128], jnp.where(group == 1, wide[:, 128:256], wide[:, 256:])
+    ).astype(BF)
     saved_ref[:, :C] = normed
     saved_ref[:, C:2 * C] = attended
     for n in range(3):
         saved_ref[:, (2 + n) * C:(3 + n) * C] = parts[n]
 
 
-def row_forward_kernel(*refs):
-    gains, w_qkv, saved_ref, probs_ref, x_ref = refs[8:]
-    me = lax.axis_index("gy")
-    for step in range(8):
-        x_ref[place(me ^ step, 32), :] = refs[step][...]
-    normed, queries, keys, values, attended = forward(1, x_ref[:, :C], gains[1:2, :], w_qkv[0], probs_ref)
+def row_forward_kernel(x, gains, w_qkv, saved_ref, probs_ref):
+    normed, queries, keys, values, attended = forward(1, x[...], gains[1:2, :], w_qkv[0], probs_ref)
     for n, v in enumerate((normed, attended, queries, keys, values)):
         saved_ref[:, n * C:(n + 1) * C] = v
 
 
 def row_backward_kernel(x, got, saved, probs, gains, w_qkv, w_out, from_cols, order, both_ref, parts_ref, stream_ref):
-    stream = mm(from_cols[...], got[...]).astype(BF)
+    group = message_group()
+    arrived = got[...].astype(F32)
+    wide = jnp.concatenate([jnp.where(group == g, arrived, 0.0).astype(BF) for g in range(3)], axis=1)
+    stream = mm(from_cols[...], wide).astype(BF)
     stream_ref[...] = stream
     parts = backward_attention(
         stream, w_out[0], saved[:, 2 * C:3 * C], saved[:, 3 * C:4 * C], saved[:, 4 * C:], probs
@@ -291,6 +296,10 @@
     return array, pl.BlockSpec((1,) + array.shape[1:], lambda g: (layer, 0, 0))
 
 
+def rows_of(array, first, count):
+    return array, pl.BlockSpec((count,) + array.shape[1:], lambda g: (first, 0, 0))
+
+
 def columns(array, first, count):
     return array, pl.BlockSpec((array.shape[0], count), lambda g: (0, first))
 
@@ -303,7 +312,7 @@
     return array, pl.BlockSpec(memory_space=pl.ANY)
 
 
-def call(kernel, ins, outs, scratch=(), flops=5e9):
+def call(kernel, ins, outs, scratch=(), flops=5e9, vmem=VMEM):
     ins = [a if isinstance(a, tuple) else (a, whole(a.shape)) for a in ins]
     return pl.pallas_call(
         kernel,
@@ -312,7 +321,7 @@
         out_specs=[whole(s) for s, _ in outs],
         out_shape=[jax.ShapeDtypeStruct(s, d) for s, d in outs],
         scratch_shapes=list(scratch),
-        compiler_params=pltpu.CompilerParams(vmem_limit_bytes=VMEM),
+        compiler_params=pltpu.CompilerParams(vmem_limit_bytes=vmem),
         cost_estimate=pl.CostEstimate(flops=int(flops), bytes_accessed=10_000, transcendentals=0),
     )(*[a for a, _ in ins])
 
@@ -341,28 +350,24 @@
     pairs = ((T, 2 * C), BF)
     terms = [((4, 192, C), BF), ((4, 192, C), BF)]
 
-    first, *moving = call(
-        centre_kernel,
-        [saved_codes.reshape(3, T, C), jnp.transpose(saved_scales, (0, 4, 1, 2, 3)).reshape(9, 16, 16), cot, to_rows],
-        [pairs] + [((32, 2 * C), BF)] * 8,
-        [pltpu.VMEM(*pairs)],
-    )
+    codes = saved_codes.reshape(3, T, C)
+    scales = jnp.transpose(saved_scales, (0, 4, 1, 2, 3)).reshape(9, 16, 16)
+    (first,) = call(first_kernel, [of_layer(codes, 2), rows_of(scales, 2, 3), cot], [pairs])
     x2 = lax.all_to_all(first.reshape(8, 32, 2 * C), "gx", 0, 0, tiled=True).reshape(T, 2 * C)
-    moving = moving[:1] + [
-        lax.ppermute(moving[step], "gy", [(j, j ^ step) for j in range(8)]) for step in range(1, 8)
-    ]
+    (second,) = call(second_kernel, [rows_of(codes, 0, 2), rows_of(scales, 0, 6), to_rows], [pairs])
+    x1 = lax.all_to_all(second.reshape(8, 32, 2 * C), "gy", 0, 0, tiled=True).reshape(T, 2 * C)
     stream2, saved2 = call(
         column_kernel,
-        [x2, gains, of_layer(w_qkv, 2), of_layer(w_out, 2), to_cols] + [after(m) for m in moving[1:]],
-        [((2 * T, C), BF), ((T, 5 * C), BF)],
+        [x2, gains, of_layer(w_qkv, 2), of_layer(w_out, 2), to_cols],
+        [((4 * T, 128), BF), ((T, 5 * C), BF)],
         [pltpu.VMEM(*probs_shape)],
     )
-    got2 = lax.all_to_all(stream2.reshape(64, 8, C), ("gy", "gx"), 0, 0, tiled=True).reshape(2 * T, C)
+    got2 = lax.all_to_all(stream2.reshape(64, 16, 128), ("gy", "gx"), 0, 0, tiled=True).reshape(4 * T, 128)
     keep2, send2 = call(column_weight_kernel, [saved2, columns(x2, 1, C)], terms)
-    saved1, probs1, x1 = call(
+    saved1, probs1 = call(
         row_forward_kernel,
-        moving + [gains, of_layer(w_qkv, 1)],
-        [((T, 5 * C), BF), probs_shape, pairs],
+        [columns(x1, 0, C), gains, of_layer(w_qkv, 1)],
+        [((T, 5 * C), BF), probs_shape],
     )
     both, parts1, stream2 = call(
         row_backward_kernel,
@@ -387,7 +392,7 @@
     )
     rows = lax.all_to_all(rows.reshape(32, 8, MAIN), ("gz", "gx"), 0, 0, tiled=True)
     (grad,) = call(home_kernel, [grad, to_home], [tokens])
-    (weight_grads,) = call(last_sum_kernel, [rows], [((6, 3 * C), F32)])
+    (weight_grads,) = call(last_sum_kernel, [rows], [((6, 3 * C), F32)], vmem=16 << 20)
     return grad.reshape(cotangent.shape), weight_grads
 
 

time: 138 us -> 134 us (0.971)
  starting transfers between devices: 55.2 us -> 53.2 us
    ppermute x7 -> x0, starting transfers between devices: 8.89 us -> none  [per_device(): lax.ppermute(moving[step], 'gy', [(j, j ^ step) for j in range(8)])]
    all_to_all x1 -> x2, starting transfers between devices: 7.06 us -> 11.9 us  [the longest x1 6.91 us: per_device(): lax.all_to_all(second.reshape(8, 32, 2 * C), 'gy', 0, 0, tiled=True)]
    ppermute x7 -> x0, waiting for transfers between devices: 4.68 us -> none  [per_device(): lax.ppermute(moving[step], 'gy', [(j, j ^ step) for j in range(8)])]
    all_to_all x1, waiting for transfers between devices: 0.01 us -> 4.27 us  [per_device(): lax.all_to_all(first.reshape(8, 32, 2 * C), 'gx', 0, 0, tiled=True)]
    all_to_all x1, starting transfers between devices: 8.35 us -> 10 us  [per_device(): lax.all_to_all(grad.reshape(32, 8, C), ('gz', 'gy'), 0, 0, tiled=True)]
    unnamed x52 -> x38, local copies, waits for them, and re-layouts: 3.76 us -> 2.51 us
    pallas_call x10 -> x11, Pallas kernels: 41.7 us -> 42.7 us  [call(): pl.pallas_call(kernel, grid=(1,), in_specs=[spec for _, spec in ins], out...]
  transfers between devices with their start and end apart: 24 -> 18, of which waited for: 10 -> 8; matrix products, arithmetic and copies ran while one was open for 1% -> 1% of each run, Pallas kernels for 22% -> 30%
where the time goes in v1:
time: 134 us; the launch traced here: 133 us
  starting transfers between devices  53.2 us (40%)
  Pallas kernels  42.7 us (32%)
  waiting for transfers between devices  32.4 us (24%)
  local copies, waits for them, and re-layouts  2.51 us (2%)
  other arithmetic  1.59 us (1%)
    pallas_call x11, Pallas kernels, call(): pl.pallas_call(kernel, grid=(1,), in_specs=[spec for _, spec in ins], out...  42.7 us
    all_to_all x1, waiting for transfers between devices, per_device(): lax.all_to_all(rows.reshape(32, 8, MAIN), ('gz', 'gx'), 0, 0, tiled=True)  13.6 us
    all_to_all x1, starting transfers between devices, per_device(): lax.all_to_all(grad.reshape(32, 8, C), ('gz', 'gy'), 0, 0, tiled=True)  10 us
    ppermute x9, starting transfers between devices, reduce_rows(): lax.ppermute(add(keep[s:s + 1], first[s:s + 1]), 'gy', [(j, (j + 2 * s) %...  8.7 us
    all_to_all x1, starting transfers between devices, per_device(): lax.all_to_all(both.reshape(4, 64, 2 * C), 'gz', 0, 0, tiled=True)  7.28 us
    all_to_all x1, waiting for transfers between devices, per_device(): lax.all_to_all(grad.reshape(32, 8, C), ('gz', 'gy'), 0, 0, tiled=True)  6.93 us
    all_to_all x1, starting transfers between devices, per_device(): lax.all_to_all(second.reshape(8, 32, 2 * C), 'gy', 0, 0, tiled=True)  6.91 us
    all_to_all x1, starting transfers between devices, per_device(): lax.all_to_all(first.reshape(8, 32, 2 * C), 'gx', 0, 0, tiled=True)  6.37 us
  transfers between devices with their start and end apart: 18, of which 8 were waited for; matrix products, arithmetic and copies ran while one was open for 1% of the time, Pallas kernels for 30%

profile of v1, /device:TPU:1, one launch (start us, length us, event | category | flops | bytes accessed | tf_op | source)
XLA Modules:
  0.0 133.2 jit_solution(10959869524652918975)
XLA Ops:
  0.6 2.2 %shard_map.123 = bf16[256,768]{1,0:T(8,128)(2,1)} custom-call(bf16[3,256,384]{2,1,0:T(8,128)(2,1)} %bitcast.29, bf16[9,16,16]{2,1,0:T(8,128)(2,1)} %bitcast.32, bf16[256,384]{1,0:T(8,128)(2,1)} %bitcast.31), custom_call_target="tpu_custom_call" | custom-call | flops 5000000000 | bytes 10000 | tf_op jit(solution)/shard_map/pallas_call | solution.py:317
  2.8 6.4 %all-to-all-start.1 = ((bf16[8,32,768]{2,1,0:T(8,128)(2,1)}), bf16[8,32,768]{2,1,0:T(8,128)(2,1)S(1)}, u32[]{:S(2)}, u32[]{:S(2)}) async-start(bf16[8,32,768]{2,1,0:T(8,128)(2,1)} %bitcast.25), calls=%async_computation.1 | async-start | bytes 786432 | tf_op jit(solution)/shard_map/all_to_all | solution.py:356
  9.2 2.5 %shard_map.122 = bf16[256,768]{1,0:T(8,128)(2,1)} custom-call(bf16[3,256,384]{2,1,0:T(8,128)(2,1)} %bitcast.30, bf16[9,16,16]{2,1,0:T(8,128)(2,1)} %bitcast.33, bf16[256,256]{1,0:T(8,128)(2,1)} %constant.10.clone.order), custom_call_target="tpu_custom_call" | custom-call | flops 5000000000 | bytes 10000 | tf_op jit(solution)/shard_map/pallas_call | solution.py:317
  11.7 4.3 %all-to-all-done.1 = bf16[8,32,768]{2,1,0:T(8,128)(2,1)S(1)} async-done(((bf16[8,32,768]{2,1,0:T(8,128)(2,1)}), bf16[8,32,768]{2,1,0:T(8,128)(2,1)S(1)}, u32[]{:S(2)}, u32[]{:S(2)}) %all-to-all-start.1) | async-done | bytes 393248 | tf_op jit(solution)/shard_map/all_to_all | solution.py:356
  16.0 6.9 %all-to-all-start = ((bf16[8,32,768]{2,1,0:T(8,128)(2,1)}), bf16[8,32,768]{2,1,0:T(8,128)(2,1)S(1)}, u32[]{:S(2)}, u32[]{:S(2)}) async-start(bf16[8,32,768]{2,1,0:T(8,128)(2,1)} %bitcast.24), calls=%async_computation | async-start | bytes 786432 | tf_op jit(solution)/shard_map/all_to_all | solution.py:358
  22.9 6.6 %shard_map.124 = (bf16[1024,128]{1,0:T(8,128)(2,1)}, bf16[256,1920]{1,0:T(8,128)(2,1)}) custom-call(bf16[256,768]{1,0:T(8,128)(2,1)} %bitcast.22, f32[3,384]{1,0:T(4,128)} %gains.7, bf16[3,384,1152]{2,1,0:T(8,128)(2,1)} %w_qkv.7, bf16[3,384,384]{2,1,0:T(8,128)(2,1)} %w_out.5, bf16[1024,256]{1,0:T(8,128)(2,1)} %constant.11.clone.order), custom_call_target="tpu_custom_call" | custom-call | flops 5000000000 | bytes 10000 | tf_op jit(solution)/shard_map/pallas_call | solution.py:317
  29.5 1.5 %all-to-all-done = bf16[8,32,768]{2,1,0:T(8,128)(2,1)S(1)} async-done(((bf16[8,32,768]{2,1,0:T(8,128)(2,1)}), bf16[8,32,768]{2,1,0:T(8,128)(2,1)S(1)}, u32[]{:S(2)}, u32[]{:S(2)}) %all-to-all-start) | async-done | bytes 393248 | tf_op jit(solution)/shard_map/all_to_all | solution.py:358
  31.0 5.0 %all-to-all-start.2 = ((bf16[64,16,128]{2,1,0:T(8,128)(2,1)}), bf16[64,16,128]{2,1,0:T(8,128)(2,1)S(1)}, u32[]{:S(2)}, u32[]{:S(2)}) async-start(bf16[64,16,128]{2,1,0:T(8,128)(2,1)} %bitcast.27), calls=%async_computation.2 | async-start | bytes 524288 | tf_op jit(solution)/shard_map/all_to_all | solution.py:365
  36.0 3.7 %shard_map.127 = (bf16[4,192,384]{2,1,0:T(8,128)(2,1)}, bf16[4,192,384]{2,1,0:T(8,128)(2,1)}) custom-call(bf16[256,1920]{1,0:T(8,128)(2,1)} %get-tuple-element.20.saved, bf16[256,768]{1,0:T(8,128)(2,1)} %bitcast.23), custom_call_target="tpu_custom_call" | custom-call | flops 5000000000 | bytes 10000 | tf_op jit(solution)/shard_map/pallas_call | solution.py:317
  39.7 0.0 copy-done.1
  39.8 0.5 collective-permute-start
  40.3 4.2 %shard_map.125 = (bf16[256,1920]{1,0:T(8,128)(2,1)}, bf16[6,256,256]{2,1,0:T(8,128)(2,1)}) custom-call(bf16[256,768]{1,0:T(8,128)(2,1)} %bitcast.20, f32[3,384]{1,0:T(4,128)} %gains.7, bf16[3,384,1152]{2,1,0:T(8,128)(2,1)} %w_qkv.7), custom_call_target="tpu_custom_call" | custom-call | flops 5000000000 | bytes 10000 | tf_op jit(solution)/shard_map/pallas_call | solution.py:317
  44.5 1.2 all-to-all-done.2
  45.7 0.7 copy-done.8
  46.4 6.0 %shard_map.126 = (bf16[256,768]{1,0:T(8,128)(2,1)}, bf16[256,1152]{1,0:T(8,128)(2,1)}, bf16[256,384]{1,0:T(8,128)(2,1)}) custom-call(bf16[256,768]{1,0:T(8,128)(2,1)} %bitcast.21, bf16[1024,128]{1,0:T(8,128)(2,1)} %bitcast.26, bf16[256,1920]{1,0:T(8,128)(2,1)} %get-tuple-element.17.saved, bf16[6,256,256]{2,1,0:T(8,128)(2,1)} %get-tuple-element.18.probs, ...), custom_call_target="tpu_custom_call" | custom-call | flops 5000000000 | bytes 10000 | tf_op jit(solution)/shard_map/pallas_call | solution.py:317
  52.4 7.3 %all-to-all-start.3 = ((bf16[4,64,768]{2,1,0:T(8,128)(2,1)}), bf16[4,64,768]{2,1,0:T(8,128)(2,1)S(1)}, u32[]{:S(2)}, u32[]{:S(2)}) async-start(bf16[4,64,768]{2,1,0:T(8,128)(2,1)} %bitcast.19), calls=%async_computation.3 | async-start | bytes 786432 | tf_op jit(solution)/shard_map/all_to_all | solution.py:377
  59.7 0.0 collective-permute-done.refs_11_
  59.7 0.1 add_convert_fusion.6
  59.8 1.6 %collective-permute-start.3 = (bf16[1,192,384]{2,1,0:T(8,128)(2,1)S(1)}, bf16[1,192,384]{2,1,0:T(8,128)(2,1)S(1)}, u32[]{:S(2)}, u32[]{:S(2)}) collective-permute-start(bf16[1,192,384]{2,1,0:T(8,128)(2,1)S(1)} %get-tuple-element.36), channel_id=1, source_target_pairs={{0,48},{8,56},{16,0},{24,8},{32,16},{40,24},{48,32},{56,40},{1,49}... | collective-permute-start | bytes 442376 | tf_op jit(solution)/shard_map/ppermute | solution.py:339
  61.4 0.4 collective-permute-start.2
  61.8 0.7 collective-permute-start.1
  62.4 3.8 %shard_map.130 = (bf16[4,192,384]{2,1,0:T(8,128)(2,1)}, bf16[4,192,384]{2,1,0:T(8,128)(2,1)}) custom-call(bf16[256,1920]{1,0:T(8,128)(2,1)} %get-tuple-element.17.saved, bf16[256,1152]{1,0:T(8,128)(2,1)} %get-tuple-element.26.parts, bf16[256,384]{1,0:T(8,128)(2,1)} %get-tuple-element.27.stream), custom_call_target="tpu_custom_call" | custom-call | flops 5000000000 | bytes 10000 | tf_op jit(solution)/shard_map/pallas_call | solution.py:317
  66.2 1.3 collective-permute-start.8
  67.5 0.0 collective-permute-done.3.refs_2_.refs_14_
  67.5 0.1 collective-permute-done.2.refs_1_.refs_13_
  67.6 4.2 %collective-permute-done.1.refs_0_.refs_12_ = bf16[1,192,384]{2,1,0:T(8,128)(2,1)S(1)} collective-permute-done((bf16[1,192,384]{2,1,0:T(8,128)(2,1)S(1)}, bf16[1,192,384]{2,1,0:T(8,128)(2,1)S(1)}, u32[]{:S(2)}, u32[]{:S(2)}) %collective-permute-start.1) | collective-permute-done | bytes 147488 | tf_op jit(solution)/shard_map/ppermute | solution.py:339
  71.8 0.0 all-to-all-done.3
  71.8 0.0 copy-done.10
  71.9 0.6 copy-done.12
  72.5 0.2 copy-done
  72.7 7.8 %shard_map.128 = (bf16[256,384]{1,0:T(8,128)(2,1)}, bf16[4,192,384]{2,1,0:T(8,128)(2,1)}, bf16[4,192,384]{2,1,0:T(8,128)(2,1)}) custom-call(bf16[256,768]{1,0:T(8,128)(2,1)} %bitcast.18, f32[3,384]{1,0:T(4,128)} %gains.7, bf16[3,384,1152]{2,1,0:T(8,128)(2,1)} %w_qkv.7, bf16[3,384,384]{2,1,0:T(8,128)(2,1)} %w_out.5, bf16[1,192,384]{2,1,0:T(8,128)(2,1)} %copy-done.12, ...), custom_call_target="tpu_custom_call" | custom-call | flops 5000000000 | bytes 10000 | tf_op jit(solution)/shard_map/pallas_call | solution.py:317
  80.5 1.5 %collective-permute-start.4 = (bf16[4,192,384]{2,1,0:T(8,128)(2,1)}, bf16[4,192,384]{2,1,0:T(8,128)(2,1)S(1)}, u32[]{:S(2)}, u32[]{:S(2)}) collective-permute-start(bf16[4,192,384]{2,1,0:T(8,128)(2,1)} %get-tuple-element.25), channel_id=1, source_target_pairs={{0,8},{8,0},{16,24},{24,16},{32,40},{40,32},{48,56},{56,48},{1,9},... | collective-permute-start | bytes 1769480 | tf_op jit(solution)/shard_map/ppermute | solution.py:337
  82.0 0.0 collective-permute-done.8.refs_6_
  82.0 0.1 add_convert_fusion
  82.1 1.4 %collective-permute-start.11 = (bf16[1,192,384]{2,1,0:T(8,128)(2,1)S(1)}, bf16[1,192,384]{2,1,0:T(8,128)(2,1)S(1)}, u32[]{:S(2)}, u32[]{:S(2)}) collective-permute-start(bf16[1,192,384]{2,1,0:T(8,128)(2,1)S(1)} %get-tuple-element.30), channel_id=1, source_target_pairs={{0,48},{8,56},{16,0},{24,8},{32,16},{40,24},{48,32},{56,40},{1,49}... | collective-permute-start | bytes 442376 | tf_op jit(solution)/shard_map/ppermute | solution.py:339
  83.5 1.3 collective-permute-start.10
  84.8 0.0 collective-permute-start.9
  84.8 0.0 collective-permute-done.4.refs_1_
  84.8 1.4 %add_convert_fusion.3 = (bf16[1,192,384]{2,1,0:T(8,128)(2,1)S(1)}, bf16[1,192,384]{2,1,0:T(8,128)(2,1)S(1)}, bf16[1,192,384]{2,1,0:T(8,128)(2,1)S(1)}) fusion(bf16[4,192,384]{2,1,0:T(8,128)(2,1)S(1)} %collective-permute-done.4.refs_1_, bf16[4,192,384]{2,1,0:T(8,128)(2,1)} %get-tuple-element.24.refs_0_), kind=kLoop, calls=%fused_computation.3 | loop fusion | flops 884736 | bytes 1327104 | tf_op jit(solution)/shard_map/convert_element_type | solution.py:333
  86.2 2.7 %collective-permute-start.7 = (bf16[1,192,384]{2,1,0:T(8,128)(2,1)S(1)}, bf16[1,192,384]{2,1,0:T(8,128)(2,1)S(1)}, u32[]{:S(2)}, u32[]{:S(2)}) collective-permute-start(bf16[1,192,384]{2,1,0:T(8,128)(2,1)S(1)} %get-tuple-element.33), channel_id=1, source_target_pairs={{0,48},{8,56},{16,0},{24,8},{32,16},{40,24},{48,32},{56,40},{1,49}... | collective-permute-start | bytes 442376 | tf_op jit(solution)/shard_map/ppermute | solution.py:339
  88.9 0.5 collective-permute-start.6
  89.4 0.0 collective-permute-done.11.refs_9_
  89.4 0.2 collective-permute-start.5
  89.6 10.0 %all-to-all-start.4 = ((bf16[32,8,384]{2,1,0:T(8,128)(2,1)}), bf16[32,8,384]{2,1,0:T(8,128)(2,1)S(1)}, u32[]{:S(2)}, u32[]{:S(2)}) async-start(bf16[32,8,384]{2,1,0:T(8,128)(2,1)} %bitcast.13), calls=%async_computation.4 | async-start | bytes 393216 | tf_op jit(solution)/shard_map/all_to_all | solution.py:387
  99.6 0.0 collective-permute-done.10.refs_8_
  99.7 0.0 collective-permute-done.9.refs_7_
  99.7 0.0 collective-permute-done.7.refs_4_
  99.7 0.0 copy-start.16
  99.7 0.0 collective-permute-done.6.refs_3_
  99.7 0.4 collective-permute-done.5.refs_2_
  100.2 0.0 copy-done.6
  100.2 0.0 copy-done.13
  100.2 0.1 copy-done.14
  100.3 0.1 copy-done.15
  100.4 0.1 copy-done.16
  100.4 0.0 copy-done.17
  100.4 0.7 copy-done.18
  101.1 3.3 %shard_map.131 = bf16[256,896]{1,0:T(8,128)(2,1)} custom-call(bf16[4,192,384]{2,1,0:T(8,128)(2,1)} %get-tuple-element.24.refs_0_, bf16[4,192,384]{2,1,0:T(8,128)(2,1)} %copy-done.7, bf16[1,192,384]{2,1,0:T(8,128)(2,1)} %copy-done.18, bf16[1,192,384]{2,1,0:T(8,128)(2,1)} %copy-done.17, bf16[1,192,384]{2,1,0:T(8,128)(2,1)} %copy-done.16, ...), custom_call_target="tpu_custom_call" | custom-call | flops 5000000000 | bytes 10000 | tf_op jit(solution)/shard_map/pallas_call | solution.py:317
  104.4 6.9 %all-to-all-done.4 = bf16[32,8,384]{2,1,0:T(8,128)(2,1)S(1)} async-done(((bf16[32,8,384]{2,1,0:T(8,128)(2,1)}), bf16[32,8,384]{2,1,0:T(8,128)(2,1)S(1)}, u32[]{:S(2)}, u32[]{:S(2)}) %all-to-all-start.4) | async-done | bytes 196640 | tf_op jit(solution)/shard_map/all_to_all | solution.py:387
  111.3 5.6 %all-to-all-start.5 = ((bf16[32,8,896]{2,1,0:T(8,128)(2,1)}), bf16[32,8,896]{2,1,0:T(8,128)(2,1)S(1)}, u32[]{:S(2)}, u32[]{:S(2)}) async-start(bf16[32,8,896]{2,1,0:T(8,128)(2,1)} %bitcast.17), calls=%async_computation.5 | async-start | bytes 917504 | tf_op jit(solution)/shard_map/all_to_all | solution.py:393
  117.0 0.0 copy-done.9
  117.0 1.9 %shard_map.129 = bf16[256,384]{1,0:T(8,128)(2,1)} custom-call(bf16[256,384]{1,0:T(8,128)(2,1)} %bitcast.28, bf16[256,256]{1,0:T(8,128)(2,1)} %constant.14.clone.order), custom_call_target="tpu_custom_call" | custom-call | flops 5000000000 | bytes 10000 | tf_op jit(solution)/shard_map/pallas_call | solution.py:317
  118.9 13.6 %all-to-all-done.5.x = bf16[32,8,896]{2,1,0:T(8,128)(2,1)S(1)} async-done(((bf16[32,8,896]{2,1,0:T(8,128)(2,1)}), bf16[32,8,896]{2,1,0:T(8,128)(2,1)S(1)}, u32[]{:S(2)}, u32[]{:S(2)}) %all-to-all-start.5) | async-done | bytes 458784 | tf_op jit(solution)/shard_map/all_to_all | solution.py:393
  132.5 0.7 shard_map.132
  (24 shorter events, 0.0 us)
Async XLA Ops:
  2.8 13.2 %all-to-all-start.1 = ((bf16[8,32,768]{2,1,0:T(8,128)(2,1)}), bf16[8,32,768]{2,1,0:T(8,128)(2,1)S(1)}, u32[]{:S(2)}, u32[]{:S(2)}) async-start(bf16[8,32,768]{2,1,0:T(8,128)(2,1)} %bitcast.25), calls=%async_computation.1 | async-start | bytes 786432 | tf_op jit(solution)/shard_map/all_to_all | solution.py:356
  16.0 6.9 %copy-start.2 = (bf16[8,32,768]{2,1,0:T(8,128)(2,1)}, bf16[8,32,768]{2,1,0:T(8,128)(2,1)S(1)}, u32[]{:S(2)}) copy-start(bf16[8,32,768]{2,1,0:T(8,128)(2,1)S(1)} %all-to-all-done.1) | copy-start | bytes 1179652
  16.0 15.0 %all-to-all-start = ((bf16[8,32,768]{2,1,0:T(8,128)(2,1)}), bf16[8,32,768]{2,1,0:T(8,128)(2,1)S(1)}, u32[]{:S(2)}, u32[]{:S(2)}) async-start(bf16[8,32,768]{2,1,0:T(8,128)(2,1)} %bitcast.24), calls=%async_computation | async-start | bytes 786432 | tf_op jit(solution)/shard_map/all_to_all | solution.py:358
  31.0 8.7 %copy-start.1 = (bf16[8,32,768]{2,1,0:T(8,128)(2,1)}, bf16[8,32,768]{2,1,0:T(8,128)(2,1)S(1)}, u32[]{:S(2)}) copy-start(bf16[8,32,768]{2,1,0:T(8,128)(2,1)S(1)} %all-to-all-done) | copy-start | bytes 1179652
  31.0 14.7 %all-to-all-start.2 = ((bf16[64,16,128]{2,1,0:T(8,128)(2,1)}), bf16[64,16,128]{2,1,0:T(8,128)(2,1)S(1)}, u32[]{:S(2)}, u32[]{:S(2)}) async-start(bf16[64,16,128]{2,1,0:T(8,128)(2,1)} %bitcast.27), calls=%async_computation.2 | async-start | bytes 524288 | tf_op jit(solution)/shard_map/all_to_all | solution.py:365
  39.8 20.0 %collective-permute-start = (bf16[4,192,384]{2,1,0:T(8,128)(2,1)}, bf16[4,192,384]{2,1,0:T(8,128)(2,1)S(1)}, u32[]{:S(2)}, u32[]{:S(2)}) collective-permute-start(bf16[4,192,384]{2,1,0:T(8,128)(2,1)} %get-tuple-element.22), channel_id=1, source_target_pairs={{0,8},{8,0},{16,24},{24,16},{32,40},{40,32},{48,56},{56,48},{1,9},... | collective-permute-start | bytes 1769480 | tf_op jit(solution)/shard_map/ppermute | solution.py:337
  45.7 0.7 copy-start.8
  46.4 13.3 %copy-start.3 = (bf16[4,192,384]{2,1,0:T(8,128)(2,1)S(1)}, bf16[4,192,384]{2,1,0:T(8,128)(2,1)}, u32[]{:S(2)}) copy-start(bf16[4,192,384]{2,1,0:T(8,128)(2,1)} %get-tuple-element.21.refs_10_) | copy-start | bytes 1769476
  52.4 19.4 %all-to-all-start.3 = ((bf16[4,64,768]{2,1,0:T(8,128)(2,1)}), bf16[4,64,768]{2,1,0:T(8,128)(2,1)S(1)}, u32[]{:S(2)}, u32[]{:S(2)}) async-start(bf16[4,64,768]{2,1,0:T(8,128)(2,1)} %bitcast.19), calls=%async_computation.3 | async-start | bytes 786432 | tf_op jit(solution)/shard_map/all_to_all | solution.py:377
  59.7 6.5 %copy-start.4 = (bf16[4,192,384]{2,1,0:T(8,128)(2,1)}, bf16[4,192,384]{2,1,0:T(8,128)(2,1)S(1)}, u32[]{:S(2)}) copy-start(bf16[4,192,384]{2,1,0:T(8,128)(2,1)S(1)} %collective-permute-done.refs_11_) | copy-start | bytes 1769476
  59.8 7.6 %collective-permute-start.3 = (bf16[1,192,384]{2,1,0:T(8,128)(2,1)S(1)}, bf16[1,192,384]{2,1,0:T(8,128)(2,1)S(1)}, u32[]{:S(2)}, u32[]{:S(2)}) collective-permute-start(bf16[1,192,384]{2,1,0:T(8,128)(2,1)S(1)} %get-tuple-element.36), channel_id=1, source_target_pairs={{0,48},{8,56},{16,0},{24,8},{32,16},{40,24},{48,32},{56,40},{1,49}... | collective-permute-start | bytes 442376 | tf_op jit(solution)/shard_map/ppermute | solution.py:339
  61.4 6.2 %collective-permute-start.2 = (bf16[1,192,384]{2,1,0:T(8,128)(2,1)S(1)}, bf16[1,192,384]{2,1,0:T(8,128)(2,1)S(1)}, u32[]{:S(2)}, u32[]{:S(2)}) collective-permute-start(bf16[1,192,384]{2,1,0:T(8,128)(2,1)S(1)} %get-tuple-element.37), channel_id=1, source_target_pairs={{0,32},{8,40},{16,48},{24,56},{32,0},{40,8},{48,16},{56,24},{1,33}... | collective-permute-start | bytes 442376 | tf_op jit(solution)/shard_map/ppermute | solution.py:339
  61.8 10.1 %collective-permute-start.1 = (bf16[1,192,384]{2,1,0:T(8,128)(2,1)S(1)}, bf16[1,192,384]{2,1,0:T(8,128)(2,1)S(1)}, u32[]{:S(2)}, u32[]{:S(2)}) collective-permute-start(bf16[1,192,384]{2,1,0:T(8,128)(2,1)S(1)} %get-tuple-element.38), channel_id=1, source_target_pairs={{0,16},{8,24},{16,32},{24,40},{32,48},{40,56},{48,0},{56,8},{1,17}... | collective-permute-start | bytes 442376 | tf_op jit(solution)/shard_map/ppermute | solution.py:339
  66.2 15.8 %collective-permute-start.8 = (bf16[4,192,384]{2,1,0:T(8,128)(2,1)}, bf16[4,192,384]{2,1,0:T(8,128)(2,1)S(1)}, u32[]{:S(2)}, u32[]{:S(2)}) collective-permute-start(bf16[4,192,384]{2,1,0:T(8,128)(2,1)} %get-tuple-element.29), channel_id=1, source_target_pairs={{0,8},{8,0},{16,24},{24,16},{32,40},{40,32},{48,56},{56,48},{1,9},... | collective-permute-start | bytes 1769480 | tf_op jit(solution)/shard_map/ppermute | solution.py:337
  67.5 4.4 %copy-start.10 = (bf16[1,192,384]{2,1,0:T(8,128)(2,1)}, bf16[1,192,384]{2,1,0:T(8,128)(2,1)S(1)}, u32[]{:S(2)}) copy-start(bf16[1,192,384]{2,1,0:T(8,128)(2,1)S(1)} %collective-permute-done.3.refs_2_.refs_14_) | copy-start | bytes 442372
  67.6 4.2 %copy-start.11 = (bf16[1,192,384]{2,1,0:T(8,128)(2,1)}, bf16[1,192,384]{2,1,0:T(8,128)(2,1)S(1)}, u32[]{:S(2)}) copy-start(bf16[1,192,384]{2,1,0:T(8,128)(2,1)S(1)} %collective-permute-done.2.refs_1_.refs_13_) | copy-start | bytes 442372
  71.8 0.7 copy-start.12
  71.8 0.8 copy-start
  72.7 9.3 %copy-start.5 = (bf16[4,192,384]{2,1,0:T(8,128)(2,1)S(1)}, bf16[4,192,384]{2,1,0:T(8,128)(2,1)}, u32[]{:S(2)}) copy-start(bf16[4,192,384]{2,1,0:T(8,128)(2,1)} %get-tuple-element.28.refs_5_) | copy-start | bytes 1769476
  80.5 4.3 %collective-permute-start.4 = (bf16[4,192,384]{2,1,0:T(8,128)(2,1)}, bf16[4,192,384]{2,1,0:T(8,128)(2,1)S(1)}, u32[]{:S(2)}, u32[]{:S(2)}) collective-permute-start(bf16[4,192,384]{2,1,0:T(8,128)(2,1)} %get-tuple-element.25), channel_id=1, source_target_pairs={{0,8},{8,0},{16,24},{24,16},{32,40},{40,32},{48,56},{56,48},{1,9},... | collective-permute-start | bytes 1769480 | tf_op jit(solution)/shard_map/ppermute | solution.py:337
  82.0 18.2 %copy-start.6 = (bf16[4,192,384]{2,1,0:T(8,128)(2,1)}, bf16[4,192,384]{2,1,0:T(8,128)(2,1)S(1)}, u32[]{:S(2)}) copy-start(bf16[4,192,384]{2,1,0:T(8,128)(2,1)S(1)} %collective-permute-done.8.refs_6_) | copy-start | bytes 1769476
  82.1 7.3 %collective-permute-start.11 = (bf16[1,192,384]{2,1,0:T(8,128)(2,1)S(1)}, bf16[1,192,384]{2,1,0:T(8,128)(2,1)S(1)}, u32[]{:S(2)}, u32[]{:S(2)}) collective-permute-start(bf16[1,192,384]{2,1,0:T(8,128)(2,1)S(1)} %get-tuple-element.30), channel_id=1, source_target_pairs={{0,48},{8,56},{16,0},{24,8},{32,16},{40,24},{48,32},{56,40},{1,49}... | collective-permute-start | bytes 442376 | tf_op jit(solution)/shard_map/ppermute | solution.py:339
  83.5 16.2 %collective-permute-start.10 = (bf16[1,192,384]{2,1,0:T(8,128)(2,1)S(1)}, bf16[1,192,384]{2,1,0:T(8,128)(2,1)S(1)}, u32[]{:S(2)}, u32[]{:S(2)}) collective-permute-start(bf16[1,192,384]{2,1,0:T(8,128)(2,1)S(1)} %get-tuple-element.31), channel_id=1, source_target_pairs={{0,32},{8,40},{16,48},{24,56},{32,0},{40,8},{48,16},{56,24},{1,33}... | collective-permute-start | bytes 442376 | tf_op jit(solution)/shard_map/ppermute | solution.py:339
  84.8 14.9 %collective-permute-start.9 = (bf16[1,192,384]{2,1,0:T(8,128)(2,1)S(1)}, bf16[1,192,384]{2,1,0:T(8,128)(2,1)S(1)}, u32[]{:S(2)}, u32[]{:S(2)}) collective-permute-start(bf16[1,192,384]{2,1,0:T(8,128)(2,1)S(1)} %get-tuple-element.32), channel_id=1, source_target_pairs={{0,16},{8,24},{16,32},{24,40},{32,48},{40,56},{48,0},{56,8},{1,17}... | collective-permute-start | bytes 442376 | tf_op jit(solution)/shard_map/ppermute | solution.py:339
  84.8 15.4 %copy-start.7 = (bf16[4,192,384]{2,1,0:T(8,128)(2,1)}, bf16[4,192,384]{2,1,0:T(8,128)(2,1)S(1)}, u32[]{:S(2)}) copy-start(bf16[4,192,384]{2,1,0:T(8,128)(2,1)S(1)} %collective-permute-done.4.refs_1_) | copy-start | bytes 1769476
  86.2 13.5 %collective-permute-start.7 = (bf16[1,192,384]{2,1,0:T(8,128)(2,1)S(1)}, bf16[1,192,384]{2,1,0:T(8,128)(2,1)S(1)}, u32[]{:S(2)}, u32[]{:S(2)}) collective-permute-start(bf16[1,192,384]{2,1,0:T(8,128)(2,1)S(1)} %get-tuple-element.33), channel_id=1, source_target_pairs={{0,48},{8,56},{16,0},{24,8},{32,16},{40,24},{48,32},{56,40},{1,49}... | collective-permute-start | bytes 442376 | tf_op jit(solution)/shard_map/ppermute | solution.py:339
  88.9 10.8 %collective-permute-start.6 = (bf16[1,192,384]{2,1,0:T(8,128)(2,1)S(1)}, bf16[1,192,384]{2,1,0:T(8,128)(2,1)S(1)}, u32[]{:S(2)}, u32[]{:S(2)}) collective-permute-start(bf16[1,192,384]{2,1,0:T(8,128)(2,1)S(1)} %get-tuple-element.34), channel_id=1, source_target_pairs={{0,32},{8,40},{16,48},{24,56},{32,0},{40,8},{48,16},{56,24},{1,33}... | collective-permute-start | bytes 442376 | tf_op jit(solution)/shard_map/ppermute | solution.py:339
  89.4 10.8 %copy-start.13 = (bf16[1,192,384]{2,1,0:T(8,128)(2,1)}, bf16[1,192,384]{2,1,0:T(8,128)(2,1)S(1)}, u32[]{:S(2)}) copy-start(bf16[1,192,384]{2,1,0:T(8,128)(2,1)S(1)} %collective-permute-done.11.refs_9_) | copy-start | bytes 442372
  89.4 10.8 %collective-permute-start.5 = (bf16[1,192,384]{2,1,0:T(8,128)(2,1)S(1)}, bf16[1,192,384]{2,1,0:T(8,128)(2,1)S(1)}, u32[]{:S(2)}, u32[]{:S(2)}) collective-permute-start(bf16[1,192,384]{2,1,0:T(8,128)(2,1)S(1)} %get-tuple-element.35), channel_id=1, source_target_pairs={{0,16},{8,24},{16,32},{24,40},{32,48},{40,56},{48,0},{56,8},{1,17}... | collective-permute-start | bytes 442376 | tf_op jit(solution)/shard_map/ppermute | solution.py:339
  89.6 21.7 %all-to-all-start.4 = ((bf16[32,8,384]{2,1,0:T(8,128)(2,1)}), bf16[32,8,384]{2,1,0:T(8,128)(2,1)S(1)}, u32[]{:S(2)}, u32[]{:S(2)}) async-start(bf16[32,8,384]{2,1,0:T(8,128)(2,1)} %bitcast.13), calls=%async_computation.4 | async-start | bytes 393216 | tf_op jit(solution)/shard_map/all_to_all | solution.py:387
  99.6 0.7 copy-start.14
  99.7 0.7 copy-start.15
  99.7 0.7 copy-start.16
  99.7 0.7 copy-start.17
  100.4 0.7 copy-start.18
  111.3 5.6 %copy-start.9 = (bf16[32,8,384]{2,1,0:T(8,128)(2,1)}, bf16[32,8,384]{2,1,0:T(8,128)(2,1)S(1)}, u32[]{:S(2)}) copy-start(bf16[32,8,384]{2,1,0:T(8,128)(2,1)S(1)} %all-to-all-done.4) | copy-start | bytes 589828
  111.3 21.2 %all-to-all-start.5 = ((bf16[32,8,896]{2,1,0:T(8,128)(2,1)}), bf16[32,8,896]{2,1,0:T(8,128)(2,1)S(1)}, u32[]{:S(2)}, u32[]{:S(2)}) async-start(bf16[32,8,896]{2,1,0:T(8,128)(2,1)} %bitcast.17), calls=%async_computation.5 | async-start | bytes 917504 | tf_op jit(solution)/shard_map/all_to_all | solution.py:393

commit v2 on v1

--- a/solution.py
+++ b/solution.py
@@ -65,6 +65,14 @@
     return low.astype(BF), (1.0 - low).astype(BF)
 
 
+def pair(a, p):
+    return a[:, 128 * p:128 * p + 128]
+
+
+def low_lanes():
+    return lax.broadcasted_iota(jnp.int32, (T, 128), 1) < 64
+
+
 def normalise(y):
     y = y.astype(F32)
     rstd = lax.rsqrt(jnp.mean(y * y, axis=-1, keepdims=True) + 1e-05)
@@ -78,49 +86,39 @@
     queries = qkv[:, :C] * jnp.asarray(0.125, BF)
     bias = line_bias(layer)
     masks = head_masks()
+    keys, values = qkv[:, C:2 * C], qkv[:, 2 * C:]
+    scores = [mm_nt(pair(queries, n // 2) * masks[n % 2], pair(keys, n // 2)) + bias for n in range(6)]
+    es = [jnp.exp(s - jnp.max(s, axis=-1, keepdims=True)) for s in scores]
+    lows = [(e * (1.0 / jnp.sum(e, axis=-1, keepdims=True))).astype(BF) for e in es]
     attended = []
     for p in range(3):
-        at = slice(128 * p, 128 * p + 128)
-        q2, k2, v2 = queries[:, at], qkv[:, C:2 * C][:, at], qkv[:, 2 * C:][:, at]
-        out = None
-        for side in range(2):
-            scores = mm_nt(q2 * masks[side], k2) + bias
-            top = jnp.max(scores, axis=-1, keepdims=True)
-            e = jnp.exp(scores - top)
-            probs = e * (1.0 / jnp.sum(e, axis=-1, keepdims=True))
-            low = probs.astype(BF)
-            probs_ref[2 * p + side] = low
-            part = mm(low, v2 * masks[side])
-            out = part if out is None else out + part
-        attended.append(out.astype(BF))
+        probs_ref[2 * p] = lows[2 * p]
+        probs_ref[2 * p + 1] = lows[2 * p + 1]
+        v2 = pair(values, p)
+        attended.append(jnp.where(low_lanes(), mm(lows[2 * p], v2), mm(lows[2 * p + 1], v2)).astype(BF))
     return normed, queries, qkv[:, C:2 * C], qkv[:, 2 * C:], jnp.concatenate(attended, axis=1)
 
 
 def backward_attention(stream, w_out, queries, keys, values, probs_ref):
     grad_attended = mm_nt(stream, w_out).astype(BF)
     masks = head_masks()
+    gs = [pair(grad_attended, n // 2) * masks[n % 2] for n in range(6)]
+    dprobs = [mm_nt(gs[n], pair(values, n // 2)) for n in range(6)]
+    dscores = []
+    for n in range(6):
+        probs = probs_ref[n].astype(F32)
+        weighted = probs * dprobs[n]
+        total = jnp.sum(weighted, axis=-1, keepdims=True)
+        dscores.append((weighted - probs * total).astype(BF))
     dq, dk, dv = [], [], []
     for p in range(3):
-        at = slice(128 * p, 128 * p + 128)
-        q2, k2, v2, g2 = queries[:, at], keys[:, at], values[:, at], grad_attended[:, at]
-        sums = None
-        for side in range(2):
-            low = probs_ref[2 * p + side]
-            g = g2 * masks[side]
-            probs = low.astype(F32)
-            dprobs = mm_nt(g, v2)
-            weighted = probs * dprobs
-            total = jnp.sum(weighted, axis=-1, keepdims=True)
-            dscore = (weighted - probs * total).astype(BF)
-            new = (
-                mm(dscore, k2 * masks[side]),
-                mm_tn(dscore, q2 * masks[side]),
-                mm_tn(low, g),
-            )
-            sums = new if sums is None else tuple(a + b for a, b in zip(sums, new))
-        dq.append((sums[0] * 0.125).astype(BF))
-        dk.append(sums[1].astype(BF))
-        dv.append(sums[2].astype(BF))
+        k2, q2 = pair(keys, p), pair(queries, p)
+        a, b = 2 * p, 2 * p + 1
+        g2 = pair(grad_attended, p)
+        low = low_lanes()
+        dq.append((jnp.where(low, mm(dscores[a], k2), mm(dscores[b], k2)) * 0.125).astype(BF))
+        dk.append(jnp.where(low, mm_tn(dscores[a], q2), mm_tn(dscores[b], q2)).astype(BF))
+        dv.append(jnp.where(low, mm_tn(probs_ref[a], g2), mm_tn(probs_ref[b], g2)).astype(BF))
     return [jnp.concatenate(d, axis=1) for d in (dq, dk, dv)]
 
 
@@ -205,20 +203,22 @@
         saved_ref[:, (2 + n) * C:(3 + n) * C] = parts[n]
 
 
-def row_forward_kernel(x, gains, w_qkv, saved_ref, probs_ref):
+def row_forward_kernel(x, gains, w_qkv, saved_ref, packed_ref, probs_ref):
     normed, queries, keys, values, attended = forward(1, x[...], gains[1:2, :], w_qkv[0], probs_ref)
-    for n, v in enumerate((normed, attended, queries, keys, values)):
-        saved_ref[:, n * C:(n + 1) * C] = v
-
-
-def row_backward_kernel(x, got, saved, probs, gains, w_qkv, w_out, from_cols, order, both_ref, parts_ref, stream_ref):
+    saved_ref[:, :C] = normed
+    saved_ref[:, C:] = attended
+    for n, v in enumerate((queries, keys, values)):
+        packed_ref[:, n * C:(n + 1) * C] = v
+
+
+def row_backward_kernel(x, got, packed, probs, gains, w_qkv, w_out, from_cols, order, both_ref, parts_ref, stream_ref):
     group = message_group()
     arrived = got[...].astype(F32)
     wide = jnp.concatenate([jnp.where(group == g, arrived, 0.0).astype(BF) for g in range(3)], axis=1)
     stream = mm(from_cols[...], wide).astype(BF)
     stream_ref[...] = stream
     parts = backward_attention(
-        stream, w_out[0], saved[:, 2 * C:3 * C], saved[:, 3 * C:4 * C], saved[:, 4 * C:], probs
+        stream, w_out[0], packed[:, :C], packed[:, C:2 * C], packed[:, 2 * C:], probs
     )
     new = backward_input(x[:, :C], stream, gains[1:2, :], w_qkv[0], parts)
     both_ref[...] = mm(order[...], jnp.concatenate([x[:, C:], new], axis=1)).astype(BF)
@@ -364,18 +364,18 @@
     )
     got2 = lax.all_to_all(stream2.reshape(64, 16, 128), ("gy", "gx"), 0, 0, tiled=True).reshape(4 * T, 128)
     keep2, send2 = call(column_weight_kernel, [saved2, columns(x2, 1, C)], terms)
-    saved1, probs1 = call(
+    saved1, packed1, probs1 = call(
         row_forward_kernel,
         [columns(x1, 0, C), gains, of_layer(w_qkv, 1)],
-        [((T, 5 * C), BF), probs_shape],
+        [pairs, ((T, 3 * C), BF), probs_shape],
     )
     both, parts1, stream2 = call(
         row_backward_kernel,
-        [x1, got2, saved1, probs1, gains, of_layer(w_qkv, 1), of_layer(w_out, 1), from_cols, to_depth],
+        [x1, got2, packed1, probs1, gains, of_layer(w_qkv, 1), of_layer(w_out, 1), from_cols, to_depth],
         [pairs, ((T, 3 * C), BF), tokens],
     )
     x0 = lax.all_to_all(both.reshape(4, 64, 2 * C), "gz", 0, 0, tiled=True).reshape(T, 2 * C)
-    keep1, send1 = call(row_weight_kernel, [columns(saved1, 0, 2 * C), parts1, stream2], terms)
+    keep1, send1 = call(row_weight_kernel, [saved1, parts1, stream2], terms)
     sums2 = reduce_rows(keep2, send2)
     sums1 = reduce_rows(keep1, send1)
     grad, keep0, send0 = call(

time: 134 us -> 131 us (0.978)
  Pallas kernels: 42.7 us -> 39 us
  waiting for transfers between devices: 32.4 us -> 35.3 us
  starting transfers between devices: 53.2 us -> 51.7 us
    pallas_call x11, Pallas kernels: 42.7 us -> 39 us  [call(): pl.pallas_call(kernel, grid=(1,), in_specs=[spec for _, spec in ins], out...]
    all_to_all x1, starting transfers between devices: 10 us -> 8.36 us  [per_device(): lax.all_to_all(grad.reshape(32, 8, C), ('gz', 'gy'), 0, 0, tiled=True)]
  transfers between devices with their start and end apart: 18 -> 18, of which waited for: 8 -> 8; matrix products, arithmetic and copies ran while one was open for 1% -> 1% of each run, Pallas kernels for 30% -> 28%
where the time goes in v2:
time: 131 us; the launch traced here: 130 us
  starting transfers between devices  51.7 us (39%)
  Pallas kernels  39 us (30%)
  waiting for transfers between devices  35.3 us (27%)
  local copies, waits for them, and re-layouts  2.15 us (2%)
  other arithmetic  1.59 us (1%)
    pallas_call x11, Pallas kernels, call(): pl.pallas_call(kernel, grid=(1,), in_specs=[spec for _, spec in ins], out...  39 us
    all_to_all x1, waiting for transfers between devices, per_device(): lax.all_to_all(rows.reshape(32, 8, MAIN), ('gz', 'gx'), 0, 0, tiled=True)  13.6 us
    all_to_all x1, starting transfers between devices, per_device(): lax.all_to_all(grad.reshape(32, 8, C), ('gz', 'gy'), 0, 0, tiled=True)  8.36 us
    ppermute x9, starting transfers between devices, reduce_rows(): lax.ppermute(add(keep[s:s + 1], first[s:s + 1]), 'gy', [(j, (j + 2 * s) %...  7.88 us
    all_to_all x1, starting transfers between devices, per_device(): lax.all_to_all(both.reshape(4, 64, 2 * C), 'gz', 0, 0, tiled=True)  7.27 us
    all_to_all x1, starting transfers between devices, per_device(): lax.all_to_all(second.reshape(8, 32, 2 * C), 'gy', 0, 0, tiled=True)  6.91 us
    all_to_all x1, waiting for transfers between devices, per_device(): lax.all_to_all(grad.reshape(32, 8, C), ('gz', 'gy'), 0, 0, tiled=True)  6.57 us
    all_to_all x1, starting transfers between devices, per_device(): lax.all_to_all(first.reshape(8, 32, 2 * C), 'gx', 0, 0, tiled=True)  6.37 us
  transfers between devices with their start and end apart: 18, of which 8 were waited for; matrix products, arithmetic and copies ran while one was open for 1% of the time, Pallas kernels for 28%

profile of v2, /device:TPU:1, one launch (start us, length us, event | category | flops | bytes accessed | tf_op | source)
XLA Modules:
  0.0 130.4 jit_solution(5870387617638844684)
XLA Ops:
  0.6 2.2 %shard_map.123 = bf16[256,768]{1,0:T(8,128)(2,1)} custom-call(bf16[3,256,384]{2,1,0:T(8,128)(2,1)} %bitcast.29, bf16[9,16,16]{2,1,0:T(8,128)(2,1)} %bitcast.32, bf16[256,384]{1,0:T(8,128)(2,1)} %bitcast.31), custom_call_target="tpu_custom_call" | custom-call | flops 5000000000 | bytes 10000 | tf_op jit(solution)/shard_map/pallas_call | solution.py:317
  2.9 6.4 %all-to-all-start.1 = ((bf16[8,32,768]{2,1,0:T(8,128)(2,1)}), bf16[8,32,768]{2,1,0:T(8,128)(2,1)S(1)}, u32[]{:S(2)}, u32[]{:S(2)}) async-start(bf16[8,32,768]{2,1,0:T(8,128)(2,1)} %bitcast.25), calls=%async_computation.1 | async-start | bytes 786432 | tf_op jit(solution)/shard_map/all_to_all | solution.py:356
  9.2 2.5 %shard_map.122 = bf16[256,768]{1,0:T(8,128)(2,1)} custom-call(bf16[3,256,384]{2,1,0:T(8,128)(2,1)} %bitcast.30, bf16[9,16,16]{2,1,0:T(8,128)(2,1)} %bitcast.33, bf16[256,256]{1,0:T(8,128)(2,1)} %constant.10.clone.order), custom_call_target="tpu_custom_call" | custom-call | flops 5000000000 | bytes 10000 | tf_op jit(solution)/shard_map/pallas_call | solution.py:317
  11.8 4.3 %all-to-all-done.1 = bf16[8,32,768]{2,1,0:T(8,128)(2,1)S(1)} async-done(((bf16[8,32,768]{2,1,0:T(8,128)(2,1)}), bf16[8,32,768]{2,1,0:T(8,128)(2,1)S(1)}, u32[]{:S(2)}, u32[]{:S(2)}) %all-to-all-start.1) | async-done | bytes 393248 | tf_op jit(solution)/shard_map/all_to_all | solution.py:356
  16.0 6.9 %all-to-all-start = ((bf16[8,32,768]{2,1,0:T(8,128)(2,1)}), bf16[8,32,768]{2,1,0:T(8,128)(2,1)S(1)}, u32[]{:S(2)}, u32[]{:S(2)}) async-start(bf16[8,32,768]{2,1,0:T(8,128)(2,1)} %bitcast.24), calls=%async_computation | async-start | bytes 786432 | tf_op jit(solution)/shard_map/all_to_all | solution.py:358
  23.0 0.0 copy-done.2
  23.0 5.5 %shard_map.124 = (bf16[1024,128]{1,0:T(8,128)(2,1)}, bf16[256,1920]{1,0:T(8,128)(2,1)}) custom-call(bf16[256,768]{1,0:T(8,128)(2,1)} %bitcast.22, f32[3,384]{1,0:T(4,128)} %gains.7, bf16[3,384,1152]{2,1,0:T(8,128)(2,1)} %w_qkv.7, bf16[3,384,384]{2,1,0:T(8,128)(2,1)} %w_out.5, bf16[1024,256]{1,0:T(8,128)(2,1)} %constant.11.clone.order), custom_call_target="tpu_custom_call" | custom-call | flops 5000000000 | bytes 10000 | tf_op jit(solution)/shard_map/pallas_call | solution.py:317
  28.5 2.5 %all-to-all-done = bf16[8,32,768]{2,1,0:T(8,128)(2,1)S(1)} async-done(((bf16[8,32,768]{2,1,0:T(8,128)(2,1)}), bf16[8,32,768]{2,1,0:T(8,128)(2,1)S(1)}, u32[]{:S(2)}, u32[]{:S(2)}) %all-to-all-start) | async-done | bytes 393248 | tf_op jit(solution)/shard_map/all_to_all | solution.py:358
  31.0 5.0 %all-to-all-start.2 = ((bf16[64,16,128]{2,1,0:T(8,128)(2,1)}), bf16[64,16,128]{2,1,0:T(8,128)(2,1)S(1)}, u32[]{:S(2)}, u32[]{:S(2)}) async-start(bf16[64,16,128]{2,1,0:T(8,128)(2,1)} %bitcast.27), calls=%async_computation.2 | async-start | bytes 524288 | tf_op jit(solution)/shard_map/all_to_all | solution.py:365
  36.0 3.8 %shard_map.127 = (bf16[4,192,384]{2,1,0:T(8,128)(2,1)}, bf16[4,192,384]{2,1,0:T(8,128)(2,1)}) custom-call(bf16[256,1920]{1,0:T(8,128)(2,1)} %get-tuple-element.21.saved, bf16[256,768]{1,0:T(8,128)(2,1)} %bitcast.23), custom_call_target="tpu_custom_call" | custom-call | flops 5000000000 | bytes 10000 | tf_op jit(solution)/shard_map/pallas_call | solution.py:317
  39.8 0.0 copy-done.1
  39.8 0.5 collective-permute-start
  40.3 3.4 %shard_map.125 = (bf16[256,768]{1,0:T(8,128)(2,1)}, bf16[256,1152]{1,0:T(8,128)(2,1)}, bf16[6,256,256]{2,1,0:T(8,128)(2,1)}) custom-call(bf16[256,768]{1,0:T(8,128)(2,1)} %bitcast.20, f32[3,384]{1,0:T(4,128)} %gains.7, bf16[3,384,1152]{2,1,0:T(8,128)(2,1)} %w_qkv.7), custom_call_target="tpu_custom_call" | custom-call | flops 5000000000 | bytes 10000 | tf_op jit(solution)/shard_map/pallas_call | solution.py:317
  43.7 2.0 %all-to-all-done.2 = bf16[64,16,128]{2,1,0:T(8,128)(2,1)S(1)} async-done(((bf16[64,16,128]{2,1,0:T(8,128)(2,1)}), bf16[64,16,128]{2,1,0:T(8,128)(2,1)S(1)}, u32[]{:S(2)}, u32[]{:S(2)}) %all-to-all-start.2) | async-done | bytes 262176 | tf_op jit(solution)/shard_map/all_to_all | solution.py:365
  45.8 0.7 copy-done.8
  46.5 5.4 %shard_map.126 = (bf16[256,768]{1,0:T(8,128)(2,1)}, bf16[256,1152]{1,0:T(8,128)(2,1)}, bf16[256,384]{1,0:T(8,128)(2,1)}) custom-call(bf16[256,768]{1,0:T(8,128)(2,1)} %bitcast.21, bf16[1024,128]{1,0:T(8,128)(2,1)} %bitcast.26, bf16[256,1152]{1,0:T(8,128)(2,1)} %get-tuple-element.18.packed, bf16[6,256,256]{2,1,0:T(8,128)(2,1)} %get-tuple-element.19.probs, ...), custom_call_target="tpu_custom_call" | custom-call | flops 5000000000 | bytes 10000 | tf_op jit(solution)/shard_map/pallas_call | solution.py:317
  51.9 7.3 %all-to-all-start.3 = ((bf16[4,64,768]{2,1,0:T(8,128)(2,1)}), bf16[4,64,768]{2,1,0:T(8,128)(2,1)S(1)}, u32[]{:S(2)}, u32[]{:S(2)}) async-start(bf16[4,64,768]{2,1,0:T(8,128)(2,1)} %bitcast.19), calls=%async_computation.3 | async-start | bytes 786432 | tf_op jit(solution)/shard_map/all_to_all | solution.py:377
  59.1 0.0 collective-permute-done.refs_11_
  59.1 0.0 copy-done.3
  59.1 0.1 add_convert_fusion.6
  59.3 0.8 collective-permute-start.3
  60.0 0.5 collective-permute-start.2
  60.5 0.6 collective-permute-start.1
  61.1 3.7 %shard_map.130 = (bf16[4,192,384]{2,1,0:T(8,128)(2,1)}, bf16[4,192,384]{2,1,0:T(8,128)(2,1)}) custom-call(bf16[256,768]{1,0:T(8,128)(2,1)} %get-tuple-element.27.saved, bf16[256,1152]{1,0:T(8,128)(2,1)} %get-tuple-element.28.parts, bf16[256,384]{1,0:T(8,128)(2,1)} %get-tuple-element.29.stream), custom_call_target="tpu_custom_call" | custom-call | flops 5000000000 | bytes 10000 | tf_op jit(solution)/shard_map/pallas_call | solution.py:317
  64.8 0.0 copy-done.4
  64.8 2.0 %collective-permute-start.8 = (bf16[4,192,384]{2,1,0:T(8,128)(2,1)}, bf16[4,192,384]{2,1,0:T(8,128)(2,1)S(1)}, u32[]{:S(2)}, u32[]{:S(2)}) collective-permute-start(bf16[4,192,384]{2,1,0:T(8,128)(2,1)} %get-tuple-element.31), channel_id=1, source_target_pairs={{0,8},{8,0},{16,24},{24,16},{32,40},{40,32},{48,56},{56,48},{1,9},... | collective-permute-start | bytes 1769480 | tf_op jit(solution)/shard_map/ppermute | solution.py:337
  66.8 0.0 collective-permute-done.3.refs_2_.refs_14_
  66.8 0.0 collective-permute-done.2.refs_1_.refs_13_
  66.8 0.0 copy-start.11
  66.8 3.1 %collective-permute-done.1.refs_0_.refs_12_ = bf16[1,192,384]{2,1,0:T(8,128)(2,1)S(1)} collective-permute-done((bf16[1,192,384]{2,1,0:T(8,128)(2,1)S(1)}, bf16[1,192,384]{2,1,0:T(8,128)(2,1)S(1)}, u32[]{:S(2)}, u32[]{:S(2)}) %collective-permute-start.1) | collective-permute-done | bytes 147488 | tf_op jit(solution)/shard_map/ppermute | solution.py:339
  69.9 1.2 all-to-all-done.3
  71.1 0.0 copy-done.10
  71.1 0.0 copy-done.11
  71.1 0.0 copy-done.12
  71.1 0.7 copy-done
  71.8 6.4 %shard_map.128 = (bf16[256,384]{1,0:T(8,128)(2,1)}, bf16[4,192,384]{2,1,0:T(8,128)(2,1)}, bf16[4,192,384]{2,1,0:T(8,128)(2,1)}) custom-call(bf16[256,768]{1,0:T(8,128)(2,1)} %bitcast.18, f32[3,384]{1,0:T(4,128)} %gains.7, bf16[3,384,1152]{2,1,0:T(8,128)(2,1)} %w_qkv.7, bf16[3,384,384]{2,1,0:T(8,128)(2,1)} %w_out.5, bf16[1,192,384]{2,1,0:T(8,128)(2,1)} %copy-done.12, ...), custom_call_target="tpu_custom_call" | custom-call | flops 5000000000 | bytes 10000 | tf_op jit(solution)/shard_map/pallas_call | solution.py:317
  78.2 1.7 %collective-permute-start.4 = (bf16[4,192,384]{2,1,0:T(8,128)(2,1)}, bf16[4,192,384]{2,1,0:T(8,128)(2,1)S(1)}, u32[]{:S(2)}, u32[]{:S(2)}) collective-permute-start(bf16[4,192,384]{2,1,0:T(8,128)(2,1)} %get-tuple-element.26), channel_id=1, source_target_pairs={{0,8},{8,0},{16,24},{24,16},{32,40},{40,32},{48,56},{56,48},{1,9},... | collective-permute-start | bytes 1769480 | tf_op jit(solution)/shard_map/ppermute | solution.py:337
  80.0 0.0 collective-permute-done.8.refs_6_
  80.0 0.0 copy-done.5
  80.0 0.1 add_convert_fusion
  80.1 1.2 collective-permute-start.11
  81.3 0.9 collective-permute-start.10
  82.2 0.6 collective-permute-start.9
  82.8 0.0 collective-permute-done.4.refs_1_
  82.8 1.4 %add_convert_fusion.3 = (bf16[1,192,384]{2,1,0:T(8,128)(2,1)S(1)}, bf16[1,192,384]{2,1,0:T(8,128)(2,1)S(1)}, bf16[1,192,384]{2,1,0:T(8,128)(2,1)S(1)}) fusion(bf16[4,192,384]{2,1,0:T(8,128)(2,1)S(1)} %collective-permute-done.4.refs_1_, bf16[4,192,384]{2,1,0:T(8,128)(2,1)} %get-tuple-element.25.refs_0_), kind=kLoop, calls=%fused_computation.3 | loop fusion | flops 884736 | bytes 1327104 | tf_op jit(solution)/shard_map/convert_element_type | solution.py:333
  84.2 2.1 %collective-permute-start.7 = (bf16[1,192,384]{2,1,0:T(8,128)(2,1)S(1)}, bf16[1,192,384]{2,1,0:T(8,128)(2,1)S(1)}, u32[]{:S(2)}, u32[]{:S(2)}) collective-permute-start(bf16[1,192,384]{2,1,0:T(8,128)(2,1)S(1)} %get-tuple-element.35), channel_id=1, source_target_pairs={{0,48},{8,56},{16,0},{24,8},{32,16},{40,24},{48,32},{56,40},{1,49}... | collective-permute-start | bytes 442376 | tf_op jit(solution)/shard_map/ppermute | solution.py:339
  86.3 0.8 collective-permute-start.6
  87.2 0.0 collective-permute-done.11.refs_9_
  87.2 0.4 collective-permute-start.5
  87.5 8.4 %all-to-all-start.4 = ((bf16[32,8,384]{2,1,0:T(8,128)(2,1)}), bf16[32,8,384]{2,1,0:T(8,128)(2,1)S(1)}, u32[]{:S(2)}, u32[]{:S(2)}) async-start(bf16[32,8,384]{2,1,0:T(8,128)(2,1)} %bitcast.13), calls=%async_computation.4 | async-start | bytes 393216 | tf_op jit(solution)/shard_map/all_to_all | solution.py:387
  95.9 0.0 collective-permute-done.10.refs_8_
  95.9 0.0 copy-start.14
  95.9 0.0 collective-permute-done.9.refs_7_
  96.0 0.0 collective-permute-done.7.refs_4_
  96.0 0.0 collective-permute-done.6.refs_3_
  96.0 1.9 %collective-permute-done.5.refs_2_ = bf16[1,192,384]{2,1,0:T(8,128)(2,1)S(1)} collective-permute-done((bf16[1,192,384]{2,1,0:T(8,128)(2,1)S(1)}, bf16[1,192,384]{2,1,0:T(8,128)(2,1)S(1)}, u32[]{:S(2)}, u32[]{:S(2)}) %collective-permute-start.5) | collective-permute-done | bytes 147488 | tf_op jit(solution)/shard_map/ppermute | solution.py:339
  97.9 0.0 copy-done.7
  98.0 0.6 copy-done.18
  98.6 3.3 %shard_map.131 = bf16[256,896]{1,0:T(8,128)(2,1)} custom-call(bf16[4,192,384]{2,1,0:T(8,128)(2,1)} %get-tuple-element.25.refs_0_, bf16[4,192,384]{2,1,0:T(8,128)(2,1)} %copy-done.7, bf16[1,192,384]{2,1,0:T(8,128)(2,1)} %copy-done.18, bf16[1,192,384]{2,1,0:T(8,128)(2,1)} %copy-done.17, bf16[1,192,384]{2,1,0:T(8,128)(2,1)} %copy-done.16, ...), custom_call_target="tpu_custom_call" | custom-call | flops 5000000000 | bytes 10000 | tf_op jit(solution)/shard_map/pallas_call | solution.py:317
  101.9 6.6 %all-to-all-done.4 = bf16[32,8,384]{2,1,0:T(8,128)(2,1)S(1)} async-done(((bf16[32,8,384]{2,1,0:T(8,128)(2,1)}), bf16[32,8,384]{2,1,0:T(8,128)(2,1)S(1)}, u32[]{:S(2)}, u32[]{:S(2)}) %all-to-all-start.4) | async-done | bytes 196640 | tf_op jit(solution)/shard_map/all_to_all | solution.py:387
  108.5 5.7 %all-to-all-start.5 = ((bf16[32,8,896]{2,1,0:T(8,128)(2,1)}), bf16[32,8,896]{2,1,0:T(8,128)(2,1)S(1)}, u32[]{:S(2)}, u32[]{:S(2)}) async-start(bf16[32,8,896]{2,1,0:T(8,128)(2,1)} %bitcast.17), calls=%async_computation.5 | async-start | bytes 917504 | tf_op jit(solution)/shard_map/all_to_all | solution.py:393
  114.2 1.9 %shard_map.129 = bf16[256,384]{1,0:T(8,128)(2,1)} custom-call(bf16[256,384]{1,0:T(8,128)(2,1)} %bitcast.28, bf16[256,256]{1,0:T(8,128)(2,1)} %constant.14.clone.order), custom_call_target="tpu_custom_call" | custom-call | flops 5000000000 | bytes 10000 | tf_op jit(solution)/shard_map/pallas_call | solution.py:317
  116.1 13.6 %all-to-all-done.5.x = bf16[32,8,896]{2,1,0:T(8,128)(2,1)S(1)} async-done(((bf16[32,8,896]{2,1,0:T(8,128)(2,1)}), bf16[32,8,896]{2,1,0:T(8,128)(2,1)S(1)}, u32[]{:S(2)}, u32[]{:S(2)}) %all-to-all-start.5) | async-done | bytes 458784 | tf_op jit(solution)/shard_map/all_to_all | solution.py:393
  129.7 0.7 shard_map.132
  (24 shorter events, 0.0 us)
Async XLA Ops:
  2.9 13.2 %all-to-all-start.1 = ((bf16[8,32,768]{2,1,0:T(8,128)(2,1)}), bf16[8,32,768]{2,1,0:T(8,128)(2,1)S(1)}, u32[]{:S(2)}, u32[]{:S(2)}) async-start(bf16[8,32,768]{2,1,0:T(8,128)(2,1)} %bitcast.25), calls=%async_computation.1 | async-start | bytes 786432 | tf_op jit(solution)/shard_map/all_to_all | solution.py:356
  16.0 6.9 %copy-start.2 = (bf16[8,32,768]{2,1,0:T(8,128)(2,1)}, bf16[8,32,768]{2,1,0:T(8,128)(2,1)S(1)}, u32[]{:S(2)}) copy-start(bf16[8,32,768]{2,1,0:T(8,128)(2,1)S(1)} %all-to-all-done.1) | copy-start | bytes 1179652
  16.0 15.0 %all-to-all-start = ((bf16[8,32,768]{2,1,0:T(8,128)(2,1)}), bf16[8,32,768]{2,1,0:T(8,128)(2,1)S(1)}, u32[]{:S(2)}, u32[]{:S(2)}) async-start(bf16[8,32,768]{2,1,0:T(8,128)(2,1)} %bitcast.24), calls=%async_computation | async-start | bytes 786432 | tf_op jit(solution)/shard_map/all_to_all | solution.py:358
  31.0 8.8 %copy-start.1 = (bf16[8,32,768]{2,1,0:T(8,128)(2,1)}, bf16[8,32,768]{2,1,0:T(8,128)(2,1)S(1)}, u32[]{:S(2)}) copy-start(bf16[8,32,768]{2,1,0:T(8,128)(2,1)S(1)} %all-to-all-done) | copy-start | bytes 1179652
  31.0 14.7 %all-to-all-start.2 = ((bf16[64,16,128]{2,1,0:T(8,128)(2,1)}), bf16[64,16,128]{2,1,0:T(8,128)(2,1)S(1)}, u32[]{:S(2)}, u32[]{:S(2)}) async-start(bf16[64,16,128]{2,1,0:T(8,128)(2,1)} %bitcast.27), calls=%async_computation.2 | async-start | bytes 524288 | tf_op jit(solution)/shard_map/all_to_all | solution.py:365
  39.8 19.3 %collective-permute-start = (bf16[4,192,384]{2,1,0:T(8,128)(2,1)}, bf16[4,192,384]{2,1,0:T(8,128)(2,1)S(1)}, u32[]{:S(2)}, u32[]{:S(2)}) collective-permute-start(bf16[4,192,384]{2,1,0:T(8,128)(2,1)} %get-tuple-element.23), channel_id=1, source_target_pairs={{0,8},{8,0},{16,24},{24,16},{32,40},{40,32},{48,56},{56,48},{1,9},... | collective-permute-start | bytes 1769480 | tf_op jit(solution)/shard_map/ppermute | solution.py:337
  45.8 0.7 copy-start.8
  46.5 12.7 %copy-start.3 = (bf16[4,192,384]{2,1,0:T(8,128)(2,1)S(1)}, bf16[4,192,384]{2,1,0:T(8,128)(2,1)}, u32[]{:S(2)}) copy-start(bf16[4,192,384]{2,1,0:T(8,128)(2,1)} %get-tuple-element.22.refs_10_) | copy-start | bytes 1769476
  51.9 19.2 %all-to-all-start.3 = ((bf16[4,64,768]{2,1,0:T(8,128)(2,1)}), bf16[4,64,768]{2,1,0:T(8,128)(2,1)S(1)}, u32[]{:S(2)}, u32[]{:S(2)}) async-start(bf16[4,64,768]{2,1,0:T(8,128)(2,1)} %bitcast.19), calls=%async_computation.3 | async-start | bytes 786432 | tf_op jit(solution)/shard_map/all_to_all | solution.py:377
  59.1 5.7 %copy-start.4 = (bf16[4,192,384]{2,1,0:T(8,128)(2,1)}, bf16[4,192,384]{2,1,0:T(8,128)(2,1)S(1)}, u32[]{:S(2)}) copy-start(bf16[4,192,384]{2,1,0:T(8,128)(2,1)S(1)} %collective-permute-done.refs_11_) | copy-start | bytes 1769476
  59.3 7.5 %collective-permute-start.3 = (bf16[1,192,384]{2,1,0:T(8,128)(2,1)S(1)}, bf16[1,192,384]{2,1,0:T(8,128)(2,1)S(1)}, u32[]{:S(2)}, u32[]{:S(2)}) collective-permute-start(bf16[1,192,384]{2,1,0:T(8,128)(2,1)S(1)} %get-tuple-element.38), channel_id=1, source_target_pairs={{0,48},{8,56},{16,0},{24,8},{32,16},{40,24},{48,32},{56,40},{1,49}... | collective-permute-start | bytes 442376 | tf_op jit(solution)/shard_map/ppermute | solution.py:339
  60.0 6.8 %collective-permute-start.2 = (bf16[1,192,384]{2,1,0:T(8,128)(2,1)S(1)}, bf16[1,192,384]{2,1,0:T(8,128)(2,1)S(1)}, u32[]{:S(2)}, u32[]{:S(2)}) collective-permute-start(bf16[1,192,384]{2,1,0:T(8,128)(2,1)S(1)} %get-tuple-element.39), channel_id=1, source_target_pairs={{0,32},{8,40},{16,48},{24,56},{32,0},{40,8},{48,16},{56,24},{1,33}... | collective-permute-start | bytes 442376 | tf_op jit(solution)/shard_map/ppermute | solution.py:339
  60.5 9.4 %collective-permute-start.1 = (bf16[1,192,384]{2,1,0:T(8,128)(2,1)S(1)}, bf16[1,192,384]{2,1,0:T(8,128)(2,1)S(1)}, u32[]{:S(2)}, u32[]{:S(2)}) collective-permute-start(bf16[1,192,384]{2,1,0:T(8,128)(2,1)S(1)} %get-tuple-element.40), channel_id=1, source_target_pairs={{0,16},{8,24},{16,32},{24,40},{32,48},{40,56},{48,0},{56,8},{1,17}... | collective-permute-start | bytes 442376 | tf_op jit(solution)/shard_map/ppermute | solution.py:339
  64.8 15.1 %collective-permute-start.8 = (bf16[4,192,384]{2,1,0:T(8,128)(2,1)}, bf16[4,192,384]{2,1,0:T(8,128)(2,1)S(1)}, u32[]{:S(2)}, u32[]{:S(2)}) collective-permute-start(bf16[4,192,384]{2,1,0:T(8,128)(2,1)} %get-tuple-element.31), channel_id=1, source_target_pairs={{0,8},{8,0},{16,24},{24,16},{32,40},{40,32},{48,56},{56,48},{1,9},... | collective-permute-start | bytes 1769480 | tf_op jit(solution)/shard_map/ppermute | solution.py:337
  66.8 4.3 %copy-start.10 = (bf16[1,192,384]{2,1,0:T(8,128)(2,1)}, bf16[1,192,384]{2,1,0:T(8,128)(2,1)S(1)}, u32[]{:S(2)}) copy-start(bf16[1,192,384]{2,1,0:T(8,128)(2,1)S(1)} %collective-permute-done.3.refs_2_.refs_14_) | copy-start | bytes 442372
  66.8 4.3 %copy-start.11 = (bf16[1,192,384]{2,1,0:T(8,128)(2,1)}, bf16[1,192,384]{2,1,0:T(8,128)(2,1)S(1)}, u32[]{:S(2)}) copy-start(bf16[1,192,384]{2,1,0:T(8,128)(2,1)S(1)} %collective-permute-done.2.refs_1_.refs_13_) | copy-start | bytes 442372
  69.9 1.2 copy-start.12
  71.1 0.7 copy-start
  71.8 8.1 %copy-start.5 = (bf16[4,192,384]{2,1,0:T(8,128)(2,1)S(1)}, bf16[4,192,384]{2,1,0:T(8,128)(2,1)}, u32[]{:S(2)}) copy-start(bf16[4,192,384]{2,1,0:T(8,128)(2,1)} %get-tuple-element.30.refs_5_) | copy-start | bytes 1769476
  78.2 4.6 %collective-permute-start.4 = (bf16[4,192,384]{2,1,0:T(8,128)(2,1)}, bf16[4,192,384]{2,1,0:T(8,128)(2,1)S(1)}, u32[]{:S(2)}, u32[]{:S(2)}) collective-permute-start(bf16[4,192,384]{2,1,0:T(8,128)(2,1)} %get-tuple-element.26), channel_id=1, source_target_pairs={{0,8},{8,0},{16,24},{24,16},{32,40},{40,32},{48,56},{56,48},{1,9},... | collective-permute-start | bytes 1769480 | tf_op jit(solution)/shard_map/ppermute | solution.py:337
  80.0 17.9 %copy-start.6 = (bf16[4,192,384]{2,1,0:T(8,128)(2,1)}, bf16[4,192,384]{2,1,0:T(8,128)(2,1)S(1)}, u32[]{:S(2)}) copy-start(bf16[4,192,384]{2,1,0:T(8,128)(2,1)S(1)} %collective-permute-done.8.refs_6_) | copy-start | bytes 1769476
  80.1 7.1 %collective-permute-start.11 = (bf16[1,192,384]{2,1,0:T(8,128)(2,1)S(1)}, bf16[1,192,384]{2,1,0:T(8,128)(2,1)S(1)}, u32[]{:S(2)}, u32[]{:S(2)}) collective-permute-start(bf16[1,192,384]{2,1,0:T(8,128)(2,1)S(1)} %get-tuple-element.32), channel_id=1, source_target_pairs={{0,48},{8,56},{16,0},{24,8},{32,16},{40,24},{48,32},{56,40},{1,49}... | collective-permute-start | bytes 442376 | tf_op jit(solution)/shard_map/ppermute | solution.py:339
  81.3 14.6 %collective-permute-start.10 = (bf16[1,192,384]{2,1,0:T(8,128)(2,1)S(1)}, bf16[1,192,384]{2,1,0:T(8,128)(2,1)S(1)}, u32[]{:S(2)}, u32[]{:S(2)}) collective-permute-start(bf16[1,192,384]{2,1,0:T(8,128)(2,1)S(1)} %get-tuple-element.33), channel_id=1, source_target_pairs={{0,32},{8,40},{16,48},{24,56},{32,0},{40,8},{48,16},{56,24},{1,33}... | collective-permute-start | bytes 442376 | tf_op jit(solution)/shard_map/ppermute | solution.py:339
  82.2 13.7 %collective-permute-start.9 = (bf16[1,192,384]{2,1,0:T(8,128)(2,1)S(1)}, bf16[1,192,384]{2,1,0:T(8,128)(2,1)S(1)}, u32[]{:S(2)}, u32[]{:S(2)}) collective-permute-start(bf16[1,192,384]{2,1,0:T(8,128)(2,1)S(1)} %get-tuple-element.34), channel_id=1, source_target_pairs={{0,16},{8,24},{16,32},{24,40},{32,48},{40,56},{48,0},{56,8},{1,17}... | collective-permute-start | bytes 442376 | tf_op jit(solution)/shard_map/ppermute | solution.py:339
  82.8 15.1 %copy-start.7 = (bf16[4,192,384]{2,1,0:T(8,128)(2,1)}, bf16[4,192,384]{2,1,0:T(8,128)(2,1)S(1)}, u32[]{:S(2)}) copy-start(bf16[4,192,384]{2,1,0:T(8,128)(2,1)S(1)} %collective-permute-done.4.refs_1_) | copy-start | bytes 1769476
  84.2 11.8 %collective-permute-start.7 = (bf16[1,192,384]{2,1,0:T(8,128)(2,1)S(1)}, bf16[1,192,384]{2,1,0:T(8,128)(2,1)S(1)}, u32[]{:S(2)}, u32[]{:S(2)}) collective-permute-start(bf16[1,192,384]{2,1,0:T(8,128)(2,1)S(1)} %get-tuple-element.35), channel_id=1, source_target_pairs={{0,48},{8,56},{16,0},{24,8},{32,16},{40,24},{48,32},{56,40},{1,49}... | collective-permute-start | bytes 442376 | tf_op jit(solution)/shard_map/ppermute | solution.py:339
  86.3 9.6 %collective-permute-start.6 = (bf16[1,192,384]{2,1,0:T(8,128)(2,1)S(1)}, bf16[1,192,384]{2,1,0:T(8,128)(2,1)S(1)}, u32[]{:S(2)}, u32[]{:S(2)}) collective-permute-start(bf16[1,192,384]{2,1,0:T(8,128)(2,1)S(1)} %get-tuple-element.36), channel_id=1, source_target_pairs={{0,32},{8,40},{16,48},{24,56},{32,0},{40,8},{48,16},{56,24},{1,33}... | collective-permute-start | bytes 442376 | tf_op jit(solution)/shard_map/ppermute | solution.py:339
  87.2 10.8 %copy-start.13 = (bf16[1,192,384]{2,1,0:T(8,128)(2,1)}, bf16[1,192,384]{2,1,0:T(8,128)(2,1)S(1)}, u32[]{:S(2)}) copy-start(bf16[1,192,384]{2,1,0:T(8,128)(2,1)S(1)} %collective-permute-done.11.refs_9_) | copy-start | bytes 442372
  87.2 10.8 %collective-permute-start.5 = (bf16[1,192,384]{2,1,0:T(8,128)(2,1)S(1)}, bf16[1,192,384]{2,1,0:T(8,128)(2,1)S(1)}, u32[]{:S(2)}, u32[]{:S(2)}) collective-permute-start(bf16[1,192,384]{2,1,0:T(8,128)(2,1)S(1)} %get-tuple-element.37), channel_id=1, source_target_pairs={{0,16},{8,24},{16,32},{24,40},{32,48},{40,56},{48,0},{56,8},{1,17}... | collective-permute-start | bytes 442376 | tf_op jit(solution)/shard_map/ppermute | solution.py:339
  87.5 20.9 %all-to-all-start.4 = ((bf16[32,8,384]{2,1,0:T(8,128)(2,1)}), bf16[32,8,384]{2,1,0:T(8,128)(2,1)S(1)}, u32[]{:S(2)}, u32[]{:S(2)}) async-start(bf16[32,8,384]{2,1,0:T(8,128)(2,1)} %bitcast.13), calls=%async_computation.4 | async-start | bytes 393216 | tf_op jit(solution)/shard_map/all_to_all | solution.py:387
  95.9 2.0 %copy-start.14 = (bf16[1,192,384]{2,1,0:T(8,128)(2,1)}, bf16[1,192,384]{2,1,0:T(8,128)(2,1)S(1)}, u32[]{:S(2)}) copy-start(bf16[1,192,384]{2,1,0:T(8,128)(2,1)S(1)} %collective-permute-done.10.refs_8_) | copy-start | bytes 442372
  95.9 2.0 %copy-start.15 = (bf16[1,192,384]{2,1,0:T(8,128)(2,1)}, bf16[1,192,384]{2,1,0:T(8,128)(2,1)S(1)}, u32[]{:S(2)}) copy-start(bf16[1,192,384]{2,1,0:T(8,128)(2,1)S(1)} %collective-permute-done.9.refs_7_) | copy-start | bytes 442372
  96.0 2.0 %copy-start.16 = (bf16[1,192,384]{2,1,0:T(8,128)(2,1)}, bf16[1,192,384]{2,1,0:T(8,128)(2,1)S(1)}, u32[]{:S(2)}) copy-start(bf16[1,192,384]{2,1,0:T(8,128)(2,1)S(1)} %collective-permute-done.7.refs_4_) | copy-start | bytes 442372
  96.0 2.0 %copy-start.17 = (bf16[1,192,384]{2,1,0:T(8,128)(2,1)}, bf16[1,192,384]{2,1,0:T(8,128)(2,1)S(1)}, u32[]{:S(2)}) copy-start(bf16[1,192,384]{2,1,0:T(8,128)(2,1)S(1)} %collective-permute-done.6.refs_3_) | copy-start | bytes 442372
  98.0 0.7 copy-start.18
  108.5 5.7 %copy-start.9 = (bf16[32,8,384]{2,1,0:T(8,128)(2,1)}, bf16[32,8,384]{2,1,0:T(8,128)(2,1)S(1)}, u32[]{:S(2)}) copy-start(bf16[32,8,384]{2,1,0:T(8,128)(2,1)S(1)} %all-to-all-done.4) | copy-start | bytes 589828
  108.5 21.2 %all-to-all-start.5 = ((bf16[32,8,896]{2,1,0:T(8,128)(2,1)}), bf16[32,8,896]{2,1,0:T(8,128)(2,1)S(1)}, u32[]{:S(2)}, u32[]{:S(2)}) async-start(bf16[32,8,896]{2,1,0:T(8,128)(2,1)} %bitcast.17), calls=%async_computation.5 | async-start | bytes 917504 | tf_op jit(solution)/shard_map/all_to_all | solution.py:393
